TPU v7x, 128 devices: a whole 4x4x4 slice. The times are simulated.
128 devices in a mesh: row: 8 (over x, y_hi), col: 16 (over y_lo, z, core).
Axes of the slice: x: 4, y: 4 (y_hi: 2, y_lo: 2; y = y_hi * 2 + y_lo), z: 4, core: 2. Of those that a mesh axis runs over, the one named last changes fastest.
Arguments:
- pair_map: bfloat16 [64, 2048, 2048], P(None, 'row', 'col'), may hold values from -6 to 6
- features: bfloat16 [2048, 256], P(('row', 'col')), may hold values from -6 to 6
- left_weight: bfloat16 [256, 32], replicated, may hold values from -0.375 to 0.375
- right_weight: bfloat16 [256, 32], replicated, may hold values from -0.375 to 0.375
- outer_weight: bfloat16 [32, 32, 64], replicated, may hold values from -0.1875 to 0.1875
- conv_weight: bfloat16 [3, 3, 64, 64], replicated, may hold values from -0.25 to 0.25
- conv_bias: float32 [64], replicated, may hold values from -4 to 4
- cotangent: bfloat16 [64, 2048, 2048], P(None, 'row', 'col'), may hold values from -6 to 6
Outputs:
- pair_out: bfloat16 [64, 2048, 2048], P(None, 'row', 'col')
- pair_grad: bfloat16 [64, 2048, 2048], P(None, 'row', 'col')
- weight_grad: float32 [3, 3, 64, 64], replicated
- feature_grad: float32 [2048, 256], P(('row', 'col'))
All inputs are finite; a program needn't handle non-finite values.
Results may differ from a plain program's by a relative error of at most 0.0059.
Values may be sent and summed in bfloat16 or wider, within the bound.
A program may use at most 320 MiB of HBM per device.

v0:
```python
import math

import jax
import jax.numpy as jnp
from jax import lax
from jax.sharding import PartitionSpec as P

REACH = 4


def padded(block, sides, width):
    for axis, dim in sides:
        count = lax.axis_size(axis)
        forward = [(i, i + 1) for i in range(count - 1)]
        backward = [(target, source) for source, target in forward]
        low = lax.ppermute(
            lax.slice_in_dim(block, block.shape[dim] - width, None, axis=dim), axis, forward
        )
        high = lax.ppermute(lax.slice_in_dim(block, 0, width, axis=dim), axis, backward)
        block = jnp.concatenate([low, block, high], axis=dim)
    return block


def tap_product(weight_tap, window):
    channel_count, height, breadth = window.shape
    flattened = window.reshape(channel_count, height * breadth)
    result = jnp.dot(weight_tap, flattened, preferred_element_type=jnp.float32)
    return result.reshape(weight_tap.shape[0], height, breadth)


def tap_outer(grad_flat, window):
    flattened = window.reshape(window.shape[0], -1)
    return lax.dot_general(
        grad_flat, flattened, (((1,), (1,)), ((), ())), preferred_element_type=jnp.float32
    )


def shards(
    pair_map, features, left_weight, right_weight, outer_weight, conv_weight, conv_bias, cotangent
):
    highest = lax.Precision.HIGHEST
    channels, tile_rows, tile_cols = pair_map.shape
    row_count = lax.axis_size("row")
    row_index = lax.axis_index("row")
    col_index = lax.axis_index("col")
    residues = tile_rows * row_count
    outer_width = left_weight.shape[1]
    whole_table = lax.all_gather(features, ("row", "col"), axis=0, tiled=True)
    row_feats = lax.dynamic_slice_in_dim(whole_table, row_index * tile_rows, tile_rows, 0)
    col_feats = lax.dynamic_slice_in_dim(whole_table, col_index * tile_cols, tile_cols, 0)
    left_rows = jnp.dot(row_feats, left_weight, preferred_element_type=jnp.float32).astype(
        jnp.bfloat16
    )
    right_rows = jnp.dot(col_feats, right_weight, preferred_element_type=jnp.float32).astype(
        jnp.bfloat16
    )
    mixing = jnp.einsum(
        "pqc,jq->pcj", outer_weight, right_rows, preferred_element_type=jnp.float32
    ).astype(jnp.bfloat16)
    update = jnp.einsum("ip,pcj->cij", left_rows, mixing, preferred_element_type=jnp.float32)
    hidden = lax.optimization_barrier((pair_map.astype(jnp.float32) + update).astype(jnp.bfloat16))
    hidden_wide = hidden.astype(jnp.float32)
    activated = jax.nn.elu(hidden_wide).astype(jnp.bfloat16)
    act_padded = padded(activated, (("row", 1), ("col", 2)), REACH)
    cot_padded = padded(cotangent, (("row", 1), ("col", 2)), REACH)
    cot_flat = cotangent.reshape(channels, -1)
    conv_total = jnp.zeros((channels, tile_rows, tile_cols), jnp.float32)
    input_grad = jnp.zeros((channels, tile_rows, tile_cols), jnp.float32)
    tap_rows = []
    for row_tap in range(3):
        forward_stack = jnp.concatenate(
            [
                act_padded[
                    :,
                    REACH * row_tap : REACH * row_tap + tile_rows,
                    REACH * col_tap : REACH * col_tap + tile_cols,
                ]
                for col_tap in range(3)
            ],
            axis=0,
        )
        forward_weight = conv_weight[row_tap].transpose(1, 0, 2).reshape(channels, 3 * channels)
        conv_total = conv_total + tap_product(forward_weight, forward_stack)
        tap_rows.append(
            tap_outer(cot_flat, forward_stack).reshape(channels, 3, channels).transpose(1, 0, 2)
        )
        back_stack = jnp.concatenate(
            [
                cot_padded[
                    :,
                    REACH * (2 - row_tap) : REACH * (2 - row_tap) + tile_rows,
                    REACH * (2 - col_tap) : REACH * (2 - col_tap) + tile_cols,
                ]
                for col_tap in range(3)
            ],
            axis=0,
        )
        back_weight = conv_weight[row_tap].transpose(2, 0, 1).reshape(channels, 3 * channels)
        input_grad = input_grad + tap_product(back_weight, back_stack)
    pair_out = (hidden_wide + conv_bias[:, None, None] + conv_total).astype(jnp.bfloat16)
    slope = jnp.where(hidden_wide > 0, 1.0, jnp.exp(jnp.minimum(hidden_wide, 0.0)))
    pair_grad = (cotangent.astype(jnp.float32) + input_grad * slope).astype(jnp.bfloat16)
    weight_grad = lax.psum(jnp.stack(tap_rows), ("row", "col")) / residues
    left_part = jnp.einsum("cij,pcj->ip", pair_grad, mixing, preferred_element_type=jnp.float32)
    mixing_part = jnp.einsum(
        "ip,cij->pcj", left_rows, pair_grad, preferred_element_type=jnp.float32
    )
    right_part = jnp.einsum(
        "pqc,pcj->jq", outer_weight.astype(jnp.float32), mixing_part, precision=highest
    )
    holder = jnp.zeros((residues, 2 * outer_width), jnp.float32)
    holder = lax.dynamic_update_slice(holder, left_part, (row_index * tile_rows, jnp.int32(0)))
    holder = lax.dynamic_update_slice(
        holder, right_part, (col_index * tile_cols, jnp.int32(outer_width))
    )
    summed = lax.psum_scatter(holder, ("row", "col"), scatter_dimension=0, tiled=True)
    left_grad = summed[:, :outer_width]
    right_grad = summed[:, outer_width:]
    feature_grad = (
        jnp.dot(
            left_grad,
            left_weight.T.astype(jnp.float32),
            precision=highest,
            preferred_element_type=jnp.float32,
        )
        + jnp.dot(
            right_grad,
            right_weight.T.astype(jnp.float32),
            precision=highest,
            preferred_element_type=jnp.float32,
        )
    ) / math.sqrt(residues)
    return (pair_out, pair_grad, weight_grad, feature_grad)


def solution(mesh):
    in_specs = (
        P(None, "row", "col"),
        P(("row", "col"), None),
        P(),
        P(),
        P(),
        P(),
        P(),
        P(None, "row", "col"),
    )
    out_specs = (P(None, "row", "col"), P(None, "row", "col"), P(), P(("row", "col"), None))
    return jax.shard_map(shards, mesh=mesh, in_specs=in_specs, out_specs=out_specs, check_vma=False)
```

profile of v0, /device:TPU:0, one launch (start us, length us, event | category | flops | bytes accessed | tf_op | source)
XLA Modules:
  0.0 1219.5 jit_solution(10022447798486511098)
XLA Ops:
  53.1 12.2 %pad_maximum_fusion.7 = (bf16[64,264,132]{1,0,2:T(8,128)(2,1)S(1)}, bf16[64,264,132]{1,0,2:T(8,128)(2,1)}) fusion(bf16[64,264,4]{1,0,2:T(8,128)(2,1)S(1)} %collective-permute-done.6, bf16[64,4,128]{1,0,2:T(8,128)(2,1)} %copy.154, bf16[64,256,128]{1,0,2:T(8,128)(2,1)} %copy.153, bf16[64,4,128]{1,0,2:T(8,128)(2,1)S(1)} %copy.152, ...), kind=kLoop, calls=%fused_computation.50 | loop fusion | flops 35684352 | bytes 13516800 | tf_op jit(solution)/shard_map/concatenate | solution.py:20
  65.3 18.6 %fusion.60 = (bf16[64,256,128]{1,0,2:T(8,128)(2,1)}, bf16[64,256,128]{1,0,2:T(8,128)(2,1)}, bf16[64,256,128]{1,0,2:T(8,128)(2,1)}, bf16[64,256,128]{1,0,2:T(8,12...) fusion(bf16[64,264,132]{1,0,2:T(8,128)(2,1)S(1)} %get-tuple-element.24, ...), kind=kLoop, calls=%fused_computation.94 | loop fusion | bytes 50331648 | tf_op jit(solution)/shard_map/slice | solution.py:89
  83.9 24.5 %fusion.16 = (bf16[192,256,128]{1,0,2:T(8,128)(2,1)}, bf16[192,256,128]{1,0,2:T(8,128)(2,1)}, bf16[192,256,128]{1,0,2:T(8,128)(2,1)}) fusion(bf16[64,256,128]{1,0,2:T(8,128)(2,1)S(1)} %copy-done.3, bf16[64,4,128]{1,0,2:T(8,128)(2,1)S(1)} %copy.152, bf16[64,256,128]{1,0,2:T(8,128)(2,1)} %get-tuple-element.64, bf16[64,256,128]{1,0,2:T(8,128)(2,1)} %get-tuple-element.38, ...), kind=kLoop, calls=%fused_computation.26 | loop fusion | flops 138412032 | bytes 67239936 | tf_op jit(solution)/shard_map/concatenate | solution.py:87
  108.4 16.8 %copy.157 = bf16[192,256,128]{2,1,0:T(8,128)(2,1)} copy(bf16[192,256,128]{1,0,2:T(8,128)(2,1)} %get-tuple-element.48) | data formatting | bytes 25165824 | tf_op jit(solution)/shard_map/concatenate | solution.py:87
  125.1 16.9 %copy.159 = bf16[192,256,128]{2,1,0:T(8,128)(2,1)} copy(bf16[192,256,128]{1,0,2:T(8,128)(2,1)} %get-tuple-element.47) | data formatting | bytes 25165824 | tf_op jit(solution)/shard_map/concatenate | solution.py:87
  142.1 15.8 %fusion.5 = f32[32768,64]{0,1:T(8,128)} fusion(bf16[64,192]{0,1:T(8,128)(2,1)S(1)} %bitcast.145, bf16[24,8,256,128]{3,2,1,0:T(8,128)(2,1)} %bitcast.139), kind=kOutput, calls=%fused_computation.14 | convolution fusion | flops 805306368 | bytes 20996096 | tf_op jit(solution)/shard_map/dot_general | solution.py:27
  157.9 32.0 %convolution_add_fusion.1 = f32[32768,64]{0,1:T(8,128)} fusion(f32[32768,64]{0,1:T(8,128)} %fusion.5, bf16[64,192]{0,1:T(8,128)(2,1)S(1)} %bitcast.148, bf16[24,8,256,128]{3,2,1,0:T(8,128)(2,1)S(1)} %bitcast.136), kind=kOutput, calls=%fused_computation.1 | convolution fusion | flops 807403520 | bytes 29384704 | tf_op jit(solution)/shard_map/dot_general | solution.py:27
  189.8 16.8 %copy.162 = bf16[192,256,128]{2,1,0:T(8,128)(2,1)} copy(bf16[192,256,128]{1,0,2:T(8,128)(2,1)} %get-tuple-element.46) | data formatting | bytes 25165824 | tf_op jit(solution)/shard_map/concatenate | solution.py:87
  206.6 15.0 %fusion.35 = f32[8,8,256,128]{3,1,2,0:T(8,128)S(1)} fusion(f32[32768,64]{0,1:T(8,128)} %convolution_add_fusion.1, bf16[64,192]{0,1:T(8,128)(2,1)S(1)} %bitcast.147, bf16[24,8,256,128]{3,2,1,0:T(8,128)(2,1)} %bitcast.137), kind=kOutput, calls=%fused_computation.53 | convolution fusion | flops 807403520 | bytes 29384704 | tf_op jit(solution)/shard_map/dot_general | solution.py:27
  241.8 9.9 fusion.25
  284.7 12.2 maximum_maximum_fusion
  302.9 11.1 fusion.59
  314.0 22.8 %fusion.20 = (bf16[192,256,128]{1,2,0:T(8,128)(2,1)}, bf16[192,256,128]{1,2,0:T(8,128)(2,1)}, bf16[192,256,128]{1,2,0:T(8,128)(2,1)}) fusion(bf16[64,4,128]{1,2,0:T(8,128)(2,1)S(1)} %copy-done.9, bf16[64,256,128]{1,2,0:T(8,128)(2,1)S(1)} %copy-done.2, bf16[64,256,128]{1,2,0:T(8,128)(2,1)} %get-tuple-element.35, bf16[64,256,128]{1,2,0:T(8,128)(2,1)S(1)} %copy-done.10, ...), kind=kLoop, calls=%fused_computation.32 | loop fusion | flops 138412032 | bytes 67239936 | tf_op jit(solution)/shard_map/concatenate | solution.py:71
  336.8 16.8 %copy.164 = bf16[192,256,128]{2,0,1:T(8,128)(2,1)} copy(bf16[192,256,128]{1,2,0:T(8,128)(2,1)} %get-tuple-element.53) | data formatting | bytes 25165824 | tf_op jit(solution)/shard_map/concatenate | solution.py:71
  363.5 16.4 %copy.167 = bf16[192,256,128]{2,0,1:T(8,128)(2,1)} copy(bf16[192,256,128]{1,2,0:T(8,128)(2,1)} %get-tuple-element.52) | data formatting | bytes 25165824 | tf_op jit(solution)/shard_map/concatenate | solution.py:71
  389.7 16.4 %copy.170 = bf16[192,256,128]{2,0,1:T(8,128)(2,1)} copy(bf16[192,256,128]{1,2,0:T(8,128)(2,1)} %get-tuple-element.51) | data formatting | bytes 25165824 | tf_op jit(solution)/shard_map/concatenate | solution.py:71
  406.1 9.9 convolution_bitcast_fusion
  425.3 16.6 %copy.141 = bf16[192,256,128]{2,1,0:T(8,128)(2,1)} copy(bf16[192,256,128]{1,2,0:T(8,128)(2,1)} %get-tuple-element.53) | data formatting | bytes 25165824 | tf_op jit(solution)/shard_map/concatenate | solution.py:71
  442.0 16.6 %copy.143 = bf16[192,256,128]{2,1,0:T(8,128)(2,1)} copy(bf16[192,256,128]{1,2,0:T(8,128)(2,1)} %get-tuple-element.52) | data formatting | bytes 25165824 | tf_op jit(solution)/shard_map/concatenate | solution.py:71
  458.6 16.8 %copy.146 = bf16[192,256,128]{2,1,0:T(8,128)(2,1)} copy(bf16[192,256,128]{1,2,0:T(8,128)(2,1)} %get-tuple-element.51) | data formatting | bytes 25165824 | tf_op jit(solution)/shard_map/concatenate | solution.py:71
  475.5 15.7 %fusion.12 = f32[32768,64]{0,1:T(8,128)} fusion(bf16[64,192]{0,1:T(8,128)(2,1)S(1)} %bitcast.146, bf16[24,8,256,128]{3,2,1,0:T(8,128)(2,1)} %bitcast.138), kind=kOutput, calls=%fused_computation.21 | convolution fusion | flops 805306368 | bytes 20996096 | tf_op jit(solution)/shard_map/dot_general | solution.py:27
  491.2 18.5 %convolution_add_fusion.3 = f32[32768,64]{0,1:T(8,128)} fusion(f32[32768,64]{0,1:T(8,128)} %fusion.12, bf16[64,192]{0,1:T(8,128)(2,1)S(1)} %bitcast.150, bf16[24,8,256,128]{3,2,1,0:T(8,128)(2,1)} %bitcast.135), kind=kOutput, calls=%fused_computation.3 | convolution fusion | flops 807403520 | bytes 29384704 | tf_op jit(solution)/shard_map/dot_general | solution.py:27
  509.8 31.9 %fusion.32 = f32[8,8,256,128]{3,1,2,0:T(8,128)} fusion(f32[32768,64]{0,1:T(8,128)} %convolution_add_fusion.3, bf16[64,192]{0,1:T(8,128)(2,1)S(1)} %bitcast.149, bf16[24,8,256,128]{3,2,1,0:T(8,128)(2,1)S(1)} %bitcast.134), kind=kOutput, calls=%fused_computation.52 | convolution fusion | flops 807403520 | bytes 29384704 | tf_op jit(solution)/shard_map/dot_general | solution.py:27
  575.6 634.5 %reduce-scatter.4.cloned.1.call-done = f32[16,64]{1,0:T(8,128)} async-done(((f32[2048,64]{1,0:T(8,128)}), f32[16,64]{1,0:T(8,128)}) %reduce-scatter.4.cloned.1.call-update) | async-done | bytes 4112
  (117 shorter events, 170.3 us)
Async XLA Ops:
  7.2 228.2 %copy-start = (bf16[256,32]{0,1:T(8,128)(2,1)S(1)}, bf16[256,32]{0,1:T(8,128)(2,1)}, u32[]{:S(2)}) copy-start(bf16[256,32]{0,1:T(8,128)(2,1)} %param.11) | copy-start | bytes 49156
  7.2 228.2 %all-gather.2.cloned.1.call-start = ((), (), s32[]{:S(2)}) async-start(), calls=%async_computation.1 | async-start | bytes 1056768 | tf_op jit(solution)/shard_map/all_gather | solution.py:48
  8.3 27.7 %collective-permute-start.4 = (bf16[64,4,128]{2,0,1:T(8,128)(2,1)S(1)}, bf16[64,4,128]{2,0,1:T(8,128)(2,1)S(1)}, u32[]{:S(2)}, u32[]{:S(2)}) collective-permute-start(bf16[64,4,128]{2,0,1:T(8,128)(2,1)S(1)} %copy.233), channel_id=1, source_target_pairs={{0,16},{16,32},{32,48},{48,64},{64,80},{80,96},{96,112},{1,17},{17... | collective-permute-start | bytes 196616 | tf_op jit(solution)/shard_map/ppermute | solution.py:16
  13.5 26.0 %collective-permute-start.5 = (bf16[64,4,128]{2,0,1:T(8,128)(2,1)S(1)}, bf16[64,4,128]{2,0,1:T(8,128)(2,1)S(1)}, u32[]{:S(2)}, u32[]{:S(2)}) collective-permute-start(bf16[64,4,128]{2,0,1:T(8,128)(2,1)S(1)} %copy.232), channel_id=1, source_target_pairs={{16,0},{32,16},{48,32},{64,48},{80,64},{96,80},{112,96},{17,1},{33... | collective-permute-start | bytes 196616 | tf_op jit(solution)/shard_map/ppermute | solution.py:19
  14.8 559.0 %all-reduce.2.cloned.1.call-start = ((), (), s32[]{:S(2)}) async-start(), calls=%async_computation.2 | async-start | bytes 589824 | tf_op jit(solution)/shard_map/psum | solution.py:103
  21.6 12.8 %copy-start.13 = (bf16[32,32,64]{2,1,0:T(8,128)(2,1)S(1)}, bf16[32,32,64]{2,1,0:T(8,128)(2,1)}, u32[]{:S(2)}) copy-start(bf16[32,32,64]{2,1,0:T(8,128)(2,1)} %param.12) | copy-start | bytes 393220
  45.1 7.9 collective-permute-start.6
  46.4 6.6 collective-permute-start.7
  65.3 18.6 %copy-start.3 = (bf16[64,256,128]{1,0,2:T(8,128)(2,1)S(1)}, bf16[64,256,128]{1,0,2:T(8,128)(2,1)}, u32[]{:S(2)}) copy-start(bf16[64,256,128]{1,0,2:T(8,128)(2,1)} %copy.153) | copy-start | bytes 12582916
  142.1 15.8 %copy-start.5 = (bf16[192,256,128]{2,1,0:T(8,128)(2,1)S(1)}, bf16[192,256,128]{2,1,0:T(8,128)(2,1)}, u32[]{:S(2)}) copy-start(bf16[192,256,128]{2,1,0:T(8,128)(2,1)} %copy.159) | copy-start | bytes 37748740
  258.1 12.8 %collective-permute-start = (bf16[64,4,128]{2,0,1:T(8,128)(2,1)S(1)}, bf16[64,4,128]{2,0,1:T(8,128)(2,1)S(1)}, u32[]{:S(2)}, u32[]{:S(2)}) collective-permute-start(bf16[64,4,128]{2,0,1:T(8,128)(2,1)S(1)} %copy.136), channel_id=1, source_target_pairs={{0,16},{16,32},{32,48},{48,64},{64,80},{80,96},{96,112},{1,17},{17... | collective-permute-start | bytes 196616 | tf_op jit(solution)/shard_map/ppermute | solution.py:16
  265.1 8.1 collective-permute-start.1
  276.9 4.5 collective-permute-start.2
  279.2 5.5 collective-permute-start.3
  302.9 11.1 copy-start.9
  302.9 11.1 copy-start.10
  416.9 793.3 %reduce-scatter.4.cloned.1.call-start = ((), (), s32[]{:S(2)}) async-start(), calls=%async_computation.3 | async-start | bytes 1056768
  458.6 16.9 %copy-start.14 = (bf16[64,3,64]{0,2,1:T(8,128)(2,1)S(1)}, bf16[64,3,64]{0,2,1:T(8,128)(2,1)}, u32[]{:S(2)}) copy-start(bf16[64,3,64]{0,2,1:T(8,128)(2,1)} %copy.142) | copy-start | bytes 73732
  475.5 15.7 %copy-start.16 = (bf16[64,3,64]{0,2,1:T(8,128)(2,1)S(1)}, bf16[64,3,64]{0,2,1:T(8,128)(2,1)}, u32[]{:S(2)}) copy-start(bf16[64,3,64]{0,2,1:T(8,128)(2,1)} %copy.144) | copy-start | bytes 73732
  491.2 18.6 %slice-start = ((s8[12582912]{0:T(1024)(128)(4,1)}), s8[4194304]{0:T(1024)(128)(4,1)S(1)}, s32[]{:S(2)}) async-start(s8[12582912]{0:T(1024)(128)(4,1)} %bitcast.132), calls=%async_computation.4 | async-start | bytes 8388608
  491.2 18.6 %slice-start.1 = ((s8[12582912]{0:T(1024)(128)(4,1)}), s8[4194304]{0:T(1024)(128)(4,1)S(1)}, s32[]{:S(2)}) async-start(s8[12582912]{0:T(1024)(128)(4,1)} %bitcast.132), calls=%async_computation.5 | async-start | bytes 8388608
  491.2 18.6 %slice-start.2 = ((s8[12582912]{0:T(1024)(128)(4,1)}), s8[4194304]{0:T(1024)(128)(4,1)S(1)}, s32[]{:S(2)}) async-start(s8[12582912]{0:T(1024)(128)(4,1)} %bitcast.132), calls=%async_computation.6 | async-start | bytes 8388608
  491.2 18.6 %copy-start.15 = (bf16[64,3,64]{0,2,1:T(8,128)(2,1)S(1)}, bf16[64,3,64]{0,2,1:T(8,128)(2,1)}, u32[]{:S(2)}) copy-start(bf16[64,3,64]{0,2,1:T(8,128)(2,1)} %copy.147) | copy-start | bytes 73732
  567.4 642.8 %copy-start.18 = (bf16[256,32]{0,1:T(8,128)(2,1)S(1)}, bf16[256,32]{0,1:T(8,128)(2,1)}, u32[]{:S(2)}) copy-start(bf16[256,32]{0,1:T(8,128)(2,1)} %param.10) | copy-start | bytes 49156
  (10 other events, 82.8 us)
Sparse Core Ops, SparseCore 0:
  14.9 66.8 all-gather.1
  417.0 153.7 all-reduce.1
  573.2 636.9 reduce-scatter.3
where the time goes:
time: 1230 us; the launch traced here: 1220 us
  waiting for transfers between devices  639 us (52%)
  local copies, waits for them, and re-layouts  276 us (22%)
  matrix products  173 us (14%)
  other arithmetic  94.9 us (8%)
  starting transfers between devices  22.4 us (2%)
  between operations  14.6 us (1%)
    unnamed x4, waiting for transfers between devices  635 us
    dot_general x6, matrix products, tap_product(): result = jnp.dot(weight_tap, flattened, preferred_element_type=jnp.float32)  129 us
    concatenate x6, local copies, waits for them, and re-layouts, shards(): jnp.concatenate([act_padded[:, REACH * row_tap:REACH * row_tap + tile_row...  99.6 us
    unnamed x58, local copies, waits for them, and re-layouts  51.1 us
    concatenate x3, local copies, waits for them, and re-layouts, shards(): jnp.concatenate([cot_padded[:, REACH * (2 - row_tap):REACH * (2 - row_tap...  50.4 us
    dot_general x3, matrix products, tap_outer(): lax.dot_general(grad_flat, flattened, (((1,), (1,)), ((), ())), preferred...  29.4 us
  transfers between devices with their start and end apart: 11, of which 3 were waited for; matrix products, arithmetic and copies ran while one was open for 31% of the time, Pallas kernels for 0%

commit v1 on v0

v1 whole, which is shorter than its diff:
```python
import functools
import math

import jax
import jax.numpy as jnp
import numpy as np
from jax import lax
from jax.experimental import pallas as pl
from jax.experimental.pallas import tpu as pltpu
from jax.sharding import PartitionSpec as P

MESH = pl.DeviceIdType.MESH
BF = jnp.bfloat16
F32 = jnp.float32
NT = (((1,), (1,)), ((), ()))
PACK = 32


def edge_selector():
    tile = np.zeros((PACK // 2, 2, PACK, 4, 2, 128), np.float32)
    for t in range(PACK // 2):
        for r in range(2):
            for q in range(4):
                tile[t, 0, 2 * t + r, q, r, q] = 1
                tile[t, 1, 2 * t + r, q, r, 124 + q] = 1
    return tile.reshape(PACK // 2 * 256, 256)


def dot(a, b, dims=None):
    if dims is None:
        return jnp.dot(a, b, preferred_element_type=F32)
    return lax.dot_general(a, b, dims, preferred_element_type=F32)


def kernel(
    nr, nc, ch, ti, outer, comm, residues,
    cot_hbm, pm_hbm, sel_hbm, bias, feat, lw, rw, ow, cw,
    po_hbm, pg_hbm, wg_out, fg_out,
    cot_n, hid_n, wide, gt, cot_t, act_t, hx, hb, sel,
    pack_acc, packs, land_row, land_col,
    lr, left_in, right_in, left, left_t, mixf, mix, wf, wb, ow_q, mgf,
    wg_acc, wgs, land_a, land_b, fin, lg_acc, lg_out, rg_out, land_l, land_r,
    in_sem, out_sem, f_send, f_recv, h_send, h_recv, w_send, w_recv, g_send, g_recv,
):
    row = lax.axis_index("row")
    col = lax.axis_index("col")
    kg = ti // PACK
    ng = ti // 4
    pitch = ti + 8
    own = lr.shape[0]
    flat = row * nc + col
    goal = flat // nr
    slot = lax.rem(flat, nr)
    up, down = lax.rem(row + nr - 1, nr), lax.rem(row + 1, nr)
    west, east = lax.rem(col + nc - 1, nc), lax.rem(col + 1, nc)
    cstep = 8
    nchunk = ch // cstep

    cot_in = [
        pltpu.make_async_copy(
            cot_hbm.at[pl.ds(k * cstep, cstep)], cot_n.at[pl.ds(k * cstep, cstep)], in_sem.at[k]
        )
        for k in range(nchunk)
    ]
    pm_in = pltpu.make_async_copy(pm_hbm, hid_n, in_sem.at[nchunk])
    sel_in = pltpu.make_async_copy(sel_hbm, sel, in_sem.at[nchunk + 1])
    for copy in cot_in:
        copy.start()
    sel_in.start()
    pm_in.start()

    def source(k):
        f = col * nr + k
        return f // nc, lax.rem(f, nc)

    if comm:
        barrier = pltpu.get_barrier_semaphore()

        def greet(r, c):
            pl.semaphore_signal(barrier, inc=1, device_id=(r, c), device_id_type=MESH)

        def greet_unless_me(r, c):
            @pl.when(jnp.logical_or(r != row, c != col))
            def _():
                greet(r, c)

        for d in range(1, nc):
            greet(row, lax.rem(col + d, nc))
        for d in range(1, nr):
            greet(lax.rem(row + d, nr), col)
        for r in (up, down):
            for c in (west, east):
                greet(r, c)
        for k in range(nr):
            greet_unless_me(k, goal)
            greet_unless_me(*source(k))
        total_greets = (nc - 1) + (nr - 1) + 4 + 2 * nr - jnp.where(goal == col, 2, 0)

    lr[...] = jnp.concatenate(
        [dot(feat[...], lw[...]), dot(feat[...], rw[...]), jnp.zeros((own, 128 - 2 * outer), F32)],
        axis=1,
    ).astype(BF)

    def remote(src, dst, ssem, rsem, dev):
        return pltpu.make_async_remote_copy(
            src_ref=src, dst_ref=dst, send_sem=ssem, recv_sem=rsem, device_id=dev, device_id_type=MESH
        )

    left_in[col] = lr[...]
    left_moves, right_moves = [], []
    if comm:
        pl.semaphore_wait(barrier, total_greets)
        for d in range(1, nc):
            move = remote(
                lr, left_in.at[col], f_send.at[d], f_recv.at[d], (row, lax.rem(col + d, nc))
            )
            move.start()
            left_moves.append(move)
        for k in range(nr):
            me = jnp.logical_and(row == k, goal == col)
            far = remote(
                lr, right_in.at[slot], f_send.at[nc + k], f_recv.at[nc + slot], (k, goal)
            )
            near = pltpu.make_async_copy(lr, right_in.at[slot], f_recv.at[nc + slot])

            @pl.when(me)
            def _():
                near.start()

            @pl.when(jnp.logical_not(me))
            def _():
                far.start()

            right_moves.append((me, far))

    for a in range(3):
        wf[a * ch : (a + 1) * ch, :] = jnp.concatenate([cw[3 * a + b] for b in range(3)], axis=1)
        wb[a * ch : (a + 1) * ch, :] = jnp.concatenate(
            [cw[3 * a + b].astype(F32).T for b in range(3)], axis=1
        ).astype(BF)
    ow_q[...] = jnp.concatenate([ow[p] for p in range(outer)], axis=1)

    for k in range(nchunk):
        cot_in[k].wait()

        @pl.loop(0, cstep)
        def _(c):
            at = pl.multiple_of((k * cstep + c) * pitch, 8)
            wide[pl.ds(at, ti), :] = cot_n[k * cstep + c].astype(F32)

    def to_rows(dst, first):
        @pl.loop(0, ti, unroll=8)
        def _(i):
            dst[first + i] = wide[pl.ds(i, ch, stride=pitch), :].astype(BF)

    to_rows(cot_t, 4)
    sel_in.wait()

    def pack_edges(src, first, which):
        pack_acc[...] = jnp.zeros_like(pack_acc)

        @pl.loop(0, PACK // 2)
        def _(t):
            rows = jnp.concatenate(
                [
                    jnp.concatenate(
                        [src[first + PACK * k + 2 * t], src[first + PACK * k + 2 * t + 1]], axis=1
                    )
                    for k in range(kg)
                ],
                axis=0,
            )
            tile = sel[pl.ds(pl.multiple_of(t * 256, 256), 256), :]
            pack_acc[...] += dot(rows, tile, NT)

        for side in range(2):
            packs[which, side] = (
                pack_acc[:, 128 * side : 128 * (side + 1)].astype(BF).reshape(kg, ch, 128)
            )

    def halo_moves(src, first, which):
        low, high = packs.at[which, 0], packs.at[which, 1]
        from_west, from_east = land_col.at[which, 0], land_col.at[which, 1]
        plan = [
            (src.at[pl.ds(first, 4)], land_row.at[which, 1], (up, col)),
            (src.at[pl.ds(first + ti - 4, 4)], land_row.at[which, 0], (down, col)),
            (low, from_east.at[pl.ds(1, kg)], (row, west)),
            (high, from_west.at[pl.ds(1, kg)], (row, east)),
            (low.at[0], from_east.at[kg + 1], (up, west)),
            (high.at[0], from_west.at[kg + 1], (up, east)),
            (low.at[kg - 1], from_east.at[0], (down, west)),
            (high.at[kg - 1], from_west.at[0], (down, east)),
        ]
        return [
            remote(s, d, h_send.at[which, m], h_recv.at[which, m], dev)
            for m, (s, d, dev) in enumerate(plan)
        ]

    pack_edges(cot_t, 4, 0)
    cot_moves = halo_moves(cot_t, 4, 0)
    if comm:
        for move in cot_moves:
            move.start()

    if comm:
        for d in range(1, nc):
            left_moves[d - 1].wait_recv()
        for k in range(nr):
            pltpu.make_async_copy(lr, right_in.at[k], f_recv.at[nc + k]).wait()
    left[...] = left_in[...].reshape(nc * own, 128)[:, :outer]
    left_t[...] = left[...].astype(F32).T.astype(BF)
    right = right_in[...].reshape(nr * own, 128)[:, outer : 2 * outer]
    step = 512
    for s in range(outer * ch // step):
        w = ow_q[:, s * step : (s + 1) * step].astype(F32).T.astype(BF)
        mixf[s * step : (s + 1) * step, :] = dot(w, right, NT).astype(BF).astype(F32)

    @pl.loop(0, ch, unroll=4)
    def _(c):
        mix[c] = mixf[pl.ds(c, outer, stride=ch), :].astype(BF)

    pm_in.wait()

    @pl.loop(0, ch, step=2)
    def _(c):
        both = jnp.concatenate([mix[c], mix[c + 1]], axis=1)
        update = dot(left[...], both)
        for k in range(2):
            hidden = (hid_n[c + k].astype(F32) + update[:, 128 * k : 128 * (k + 1)]).astype(BF)
            hid_n[c + k] = hidden
            h = hidden.astype(F32)
            at = pl.multiple_of((c + k) * pitch, 8)
            wide[pl.ds(at, ti), :] = jnp.where(h > 0, h, jnp.exp(jnp.minimum(h, 0.0)) - 1.0)

    to_rows(act_t, 8)
    for s in (0, 4, ti + 8, ti + 12):
        act_t[s : s + 4] = jnp.zeros((4, ch, 128), BF)
    pack_edges(act_t, 8, 1)
    act_moves = halo_moves(act_t, 8, 1)
    if comm:
        for move in act_moves:
            move.start()

    has_up, has_down, has_west, has_east = row > 0, row < nr - 1, col > 0, col < nc - 1

    def keep(ok, x):
        return jnp.where(ok, x, jnp.zeros_like(x))

    def unpack_edges(dst, first, which):
        dst[first : first + 4] = keep(has_up, land_row[which, 0])
        dst[first + ti + 4 : first + ti + 8] = keep(has_down, land_row[which, 1])
        for side, ok in ((0, has_west), (1, has_east)):
            lanes = slice(128 * side, 128 * (side + 1))
            hb[:ch, lanes] = keep(jnp.logical_and(ok, has_up), land_col[which, side, 0])
            for k in range(1, kg + 1):
                hb[k * ch : (k + 1) * ch, lanes] = keep(ok, land_col[which, side, k])
            hb[(kg + 1) * ch :, lanes] = keep(
                jnp.logical_and(ok, has_down), land_col[which, side, kg + 1]
            )

        @pl.loop(0, PACK // 2)
        def _(t):
            tile = sel[pl.ds(pl.multiple_of(t * 256, 256), 256), :]
            out = dot(hb[...], tile).astype(BF)
            for k in range(kg + 2):
                for r in range(2):
                    hx[PACK * k + 2 * t + r] = out[k * ch : (k + 1) * ch, 128 * r : 128 * (r + 1)]

    lane = lax.broadcasted_iota(jnp.int32, (ch, 128), 1)

    def stack(src, first, g, turned):
        rows = []
        for r in range(4):
            x = src[first + 4 * g + r]
            edge = hx[PACK - 4 + 4 * g + r]
            before = jnp.where(lane < 4, edge, pltpu.roll(x, 4, 1))
            after = jnp.where(lane >= 124, edge, pltpu.roll(x, 124, 1))
            rows.append(jnp.concatenate([after, x, before] if turned else [before, x, after], axis=0))
        return jnp.concatenate(rows, axis=1)

    def spread(part, g, order):
        for r in range(4):
            lanes = slice(128 * r, 128 * (r + 1))
            for k, a in enumerate(order):
                at = pl.ds(pl.multiple_of((4 * (g + k) + r) * ch, ch), ch)
                term = part[a * ch : (a + 1) * ch, lanes]
                if k < 2:
                    gt[at, :] += term
                else:
                    gt[at, :] = term

    if comm:
        for move in cot_moves:
            move.wait_recv()
    unpack_edges(cot_t, 0, 0)
    gt[: 8 * ch] = jnp.zeros((8 * ch, 128), F32)
    wg_acc[...] = jnp.zeros_like(wg_acc)

    @pl.loop(0, ng + 2)
    def _(g):
        terms = stack(cot_t, 0, g, True)
        spread(dot(wb[...], terms), g, (0, 1, 2))
        acts = jnp.concatenate(
            [
                jnp.concatenate([act_t[4 * (g + a) + r] for r in range(4)], axis=1)
                for a in range(3)
            ],
            axis=0,
        )
        wg_acc[...] += dot(terms, acts, NT)

    part = 2 * 3 * ch // nc
    wgs[: 3 * ch] = wg_acc[:, :128]
    wgs[3 * ch :] = jnp.concatenate([wg_acc[:, 128:], jnp.zeros((3 * ch, 256 - 3 * ch), F32)], axis=1)
    land_a[col] = wgs[pl.ds(pl.multiple_of(col * part, 8), part)]
    a_moves, b_moves, c_moves, l_moves, r_moves = [], [], [], [], []
    if comm:
        for d in range(1, nc):
            other = lax.rem(col + d, nc)
            move = remote(
                wgs.at[pl.ds(pl.multiple_of(other * part, 8), part)],
                land_a.at[col], w_send.at[d], w_recv.at[d], (row, other),
            )
            move.start()
            a_moves.append(move)

    lg_acc[...] = jnp.zeros_like(lg_acc)
    pg_out = [
        pltpu.make_async_copy(
            cot_n.at[pl.ds(k * cstep, cstep)], pg_hbm.at[pl.ds(k * cstep, cstep)], out_sem.at[k]
        )
        for k in range(nchunk)
    ]
    for k in range(nchunk):

        @pl.loop(k * cstep, (k + 1) * cstep, step=2)
        def _(c):
            grads = []
            for m in range(2):
                h = hid_n[c + m].astype(F32)
                slope = jnp.where(h > 0, 1.0, jnp.exp(jnp.minimum(h, 0.0)))
                g = gt[pl.ds(8 * ch + c + m, ti, stride=ch), :]
                pg = (cot_n[c + m].astype(F32) + g * slope).astype(BF)
                cot_n[c + m] = pg
                grads.append(pg)
            grads = jnp.concatenate(grads, axis=1)
            both = jnp.concatenate([mix[c], mix[c + 1]], axis=1)
            lg_acc[...] += dot(grads, both, NT)
            mg = dot(left_t[...], grads)
            for m in range(2):
                mgf[pl.ds(c + m, outer, stride=ch), :] = mg[:, 128 * m : 128 * (m + 1)]

        pg_out[k].start()

    mg = mgf[...]
    mg_hi = mg.astype(BF)
    mg_lo = (mg - mg_hi.astype(F32)).astype(BF)
    rg = (dot(ow_q[...], mg_hi) + dot(ow_q[...], mg_lo)).T
    rg_out[...] = rg.reshape(nr, own, outer)
    lg_out[...] = lg_acc[...].reshape(nc, own, outer)
    land_l[col] = lg_out[col]
    if comm:
        for d in range(1, nc):
            other = lax.rem(col + d, nc)
            move = remote(lg_out.at[other], land_l.at[col], g_send.at[d], g_recv.at[d], (row, other))
            move.start()
            l_moves.append(move)
        for k in range(nr):
            r, c = source(k)
            me = jnp.logical_and(r == row, c == col)
            far = remote(
                rg_out.at[k], land_r.at[row], g_send.at[nc + k], g_recv.at[nc + row], (r, c)
            )
            near = pltpu.make_async_copy(rg_out.at[k], land_r.at[row], g_recv.at[nc + row])

            @pl.when(me)
            def _():
                near.start()

            @pl.when(jnp.logical_not(me))
            def _():
                far.start()

            r_moves.append((me, far))
        for move in a_moves:
            move.wait_recv()
    total = land_a[0]
    for k in range(1, nc):
        total = total + land_a[k]
    land_b[row] = total
    if comm:
        for d in range(1, nr):
            move = remote(
                land_b.at[row], land_b.at[row], w_send.at[nc + d], w_recv.at[nc + d],
                (lax.rem(row + d, nr), col),
            )
            move.start()
            b_moves.append(move)
        for move in act_moves:
            move.wait_recv()
    unpack_edges(act_t, 4, 1)
    gt[: 8 * ch] = jnp.zeros((8 * ch, 128), F32)

    def forward(g):
        spread(dot(wf[...], stack(act_t, 4, g, False)), g, (2, 1, 0))

    forward(0)
    forward(1)
    po_out = [
        pltpu.make_async_copy(
            hid_n.at[:, pl.ds(PACK * k, PACK)], po_hbm.at[:, pl.ds(PACK * k, PACK)],
            out_sem.at[nchunk + k],
        )
        for k in range(kg)
    ]
    for k in range(kg):

        @pl.loop(8 * k + 2, 8 * k + 10)
        def _(g):
            forward(g)

        @pl.loop(0, ch, unroll=4)
        def _(c):
            conv = gt[pl.ds((8 + PACK * k) * ch + c, PACK, stride=ch), :]
            h = hid_n[c, pl.ds(PACK * k, PACK), :].astype(F32)
            hid_n[c, pl.ds(PACK * k, PACK), :] = (h + bias[c] + conv).astype(BF)

        po_out[k].start()
        if k == kg // 2 - 1:
            if comm:
                for move in b_moves:
                    move.wait_recv()
            total = land_b[0]
            for m in range(1, nr):
                total = total + land_b[m]
            fin[col] = total * (1.0 / residues)
            if comm:
                for d in range(1, nc):
                    move = remote(
                        fin.at[col], fin.at[col], w_send.at[nc + nr + d], w_recv.at[nc + nr + d],
                        (row, lax.rem(col + d, nc)),
                    )
                    move.start()
                    c_moves.append(move)

    if comm:
        for move in l_moves:
            move.wait_recv()
        for k in range(nr):
            pltpu.make_async_copy(rg_out.at[k], land_r.at[k], g_recv.at[nc + k]).wait()
    lg = land_l[0]
    for k in range(1, nc):
        lg = lg + land_l[k]
    rg = land_r[0]
    for k in range(1, nr):
        rg = rg + land_r[k]

    def exact(x, w):
        total = jnp.zeros((own, w.shape[0]), F32)
        for _ in range(3):
            head = x.astype(BF)
            total = total + dot(head, w, NT)
            x = x - head.astype(F32)
        return total

    fg_out[...] = (exact(lg, lw[...]) + exact(rg, rw[...])) * (1.0 / math.sqrt(residues))

    if comm:
        for move in c_moves:
            move.wait_recv()
    whole = fin[...].reshape(6 * ch, 128)
    for a in range(3):
        for b in range(3):
            base = 3 * ch * (a // 2) + b * ch
            at = ch * (a % 2)
            wg_out[3 * a + b] = whole[base : base + ch, at : at + ch]

    for copy in pg_out + po_out:
        copy.wait()
    if comm:
        for move in left_moves + cot_moves + act_moves + a_moves + b_moves + c_moves + l_moves:
            move.wait_send()
        for me, far in right_moves + r_moves:

            @pl.when(jnp.logical_not(me))
            def _():
                far.wait_send()


def call(nr, nc, residues, comm, pair_map, features, lw, rw, ow, cw, bias, cot):
    ch, ti, tj = pair_map.shape
    own, feat = features.shape
    outer = lw.shape[1]
    kg = ti // PACK
    part = 6 * ch // nc
    any_spec = pl.BlockSpec(memory_space=pl.ANY)
    vmem = pl.BlockSpec(memory_space=pltpu.VMEM)
    smem = pl.BlockSpec(memory_space=pltpu.SMEM)
    V = pltpu.VMEM
    dma = pltpu.SemaphoreType.DMA
    scratch = [
        V((ch, ti, tj), BF),
        V((ch, ti, tj), BF),
        V((ch * (ti + 8), 128), F32),
        V(((ti + 20) * ch, 128), F32),
        V((ti + 8, ch, 128), BF),
        V((ti + 16, ch, 128), BF),
        V(((kg + 2) * PACK, ch, 128), BF),
        V(((kg + 2) * ch, 256), BF),
        V((PACK // 2 * 256, 256), BF),
        V((kg * ch, 256), F32),
        V((2, 2, kg, ch, 128), BF),
        V((2, 2, 4, ch, 128), BF),
        V((2, 2, kg + 2, ch, 128), BF),
        V((own, 128), BF),
        V((nc, own, 128), BF),
        V((nr, own, 128), BF),
        V((ti, outer), BF),
        V((outer, ti), BF),
        V((outer * ch, 128), F32),
        V((ch, outer, 128), BF),
        V((3 * ch, 3 * ch), BF),
        V((3 * ch, 3 * ch), BF),
        V((outer, outer * ch), BF),
        V((outer * ch, 128), F32),
        V((3 * ch, 3 * ch), F32),
        V((6 * ch, 128), F32),
        V((nc, part, 128), F32),
        V((nr, part, 128), F32),
        V((nc, part, 128), F32),
        V((ti, outer), F32),
        V((nc, own, outer), F32),
        V((nr, own, outer), F32),
        V((nc, own, outer), F32),
        V((nr, own, outer), F32),
        dma((ch // 8 + 2,)),
        dma((ch // 8 + kg,)),
        dma((nc + nr,)),
        dma((nc + nr,)),
        dma((2, 8)),
        dma((2, 8)),
        dma((2 * nc + nr,)),
        dma((2 * nc + nr,)),
        dma((nc + nr,)),
        dma((nc + nr,)),
    ]
    macs = ti * tj * (27 * ch * ch + 3 * outer * ch)
    sel = jnp.asarray(edge_selector(), BF)
    out = pl.pallas_call(
        functools.partial(kernel, nr, nc, ch, ti, outer, comm, residues),
        out_shape=[
            jax.ShapeDtypeStruct((ch, ti, tj), BF),
            jax.ShapeDtypeStruct((ch, ti, tj), BF),
            jax.ShapeDtypeStruct((9, ch, ch), F32),
            jax.ShapeDtypeStruct((own, feat), F32),
        ],
        in_specs=[any_spec, any_spec, any_spec, smem] + [vmem] * 5,
        out_specs=[any_spec, any_spec, vmem, vmem],
        scratch_shapes=scratch,
        compiler_params=pltpu.CompilerParams(
            collective_id=0 if comm else None,
            has_side_effects=True,
            vmem_limit_bytes=60 * 1024 * 1024,
        ),
        cost_estimate=pl.CostEstimate(
            flops=2 * macs, bytes_accessed=8 * ch * ti * tj, transcendentals=2 * ch * ti * tj
        ),
    )(cot, pair_map, sel, bias, features, lw, rw, ow, cw.reshape(9, ch, ch))
    return out[0], out[1], out[2].reshape(3, 3, ch, ch), out[3]


def solution(mesh):
    nr, nc = mesh.shape["row"], mesh.shape["col"]

    def shards(pair_map, features, lw, rw, ow, cw, bias, cot):
        return call(
            nr, nc, pair_map.shape[1] * nr, True, pair_map, features, lw, rw, ow, cw, bias, cot
        )

    in_specs = (
        P(None, "row", "col"),
        P(("row", "col"), None),
        P(),
        P(),
        P(),
        P(),
        P(),
        P(None, "row", "col"),
    )
    out_specs = (P(None, "row", "col"), P(None, "row", "col"), P(), P(("row", "col"), None))
    return jax.shard_map(shards, mesh=mesh, in_specs=in_specs, out_specs=out_specs, check_vma=False)
```

time: 1230 us -> 112 us (0.09)
  waiting for transfers between devices: 639 us -> 0 us
  local copies, waits for them, and re-layouts: 276 us -> 11.1 us
  matrix products: 173 us -> 0 us
  Pallas kernels: 0 us -> 100 us
  other arithmetic: 94.9 us -> 0 us
  starting transfers between devices: 22.4 us -> 0 us
  between operations: 14.6 us -> 0.65 us
    unnamed x4 -> x0, waiting for transfers between devices: 635 us -> none
    dot_general x17 -> x0, matrix products: 173 us -> none  [the longest x6 129 us: tap_product(): result = jnp.dot(weight_tap, flattened, preferred_element_type=jnp.float32)]
    concatenate x9 -> x0, local copies, waits for them, and re-layouts: 150 us -> none  [the longest x6 99.6 us: shards(): jnp.concatenate([act_padded[:, REACH * row_tap:REACH * row_tap + tile_row...]
    pallas_call x0 -> x1, Pallas kernels: none -> 100 us  [call(): pl.pallas_call(functools.partial(kernel, nr, nc, ch, ti, outer, comm, res...]
    concatenate x4 -> x0, other arithmetic: 71.6 us -> none  [the longest x1 24.5 us: shards(): jnp.concatenate([cot_padded[:, REACH * (2 - row_tap):REACH * (2 - row_tap...]
    slice x8 -> x0, local copies, waits for them, and re-layouts: 43.1 us -> none  [the longest x1 18.6 us: shards(): cot_padded[:, REACH * (2 - row_tap):REACH * (2 - row_tap) + tile_rows, RE...]
    unnamed x58 -> x12, local copies, waits for them, and re-layouts: 51.1 us -> 11.1 us
    ppermute x8 -> x0, starting transfers between devices: 22.3 us -> none  [the longest x4 17.1 us: padded(): lax.ppermute(lax.slice_in_dim(block, block.shape[dim] - width, None, axis...]
  transfers between devices with their start and end apart: 11 -> 0, of which waited for: 3 -> 0; matrix products, arithmetic and copies ran while one was open for 31% -> 0% of each run, Pallas kernels for 0% -> 0%
where the time goes in v1:
time: 112 us
  Pallas kernels  100 us (89%)
  local copies, waits for them, and re-layouts  11.1 us (10%)
    pallas_call x1, Pallas kernels, call(): pl.pallas_call(functools.partial(kernel, nr, nc, ch, ti, outer, comm, res...  100 us
    unnamed x12, local copies, waits for them, and re-layouts  11.1 us

profile of v1, /device:TPU:0, one launch (start us, length us, event | category | flops | bytes accessed | tf_op | source)
XLA Modules:
  0.0 112.0 jit_solution(1659717041519591304)
XLA Ops:
  0.6 1.5 %copy.13.lw = bf16[256,32]{1,0:T(8,128)(2,1)} copy(bf16[256,32]{0,1:T(8,128)(2,1)} %param.11) | data formatting | bytes 32768 | tf_op args[2]
  2.1 1.4 %copy.14.rw = bf16[256,32]{1,0:T(8,128)(2,1)} copy(bf16[256,32]{0,1:T(8,128)(2,1)} %param.12) | data formatting | bytes 32768 | tf_op args[3]
  3.5 100.3 %shard_map.120 = (bf16[64,256,128]{2,1,0:T(8,128)(2,1)}, bf16[64,256,128]{2,1,0:T(8,128)(2,1)}, f32[9,64,64]{2,1,0:T(8,128)}, f32[16,256]{1,0:T(8,128)}) custom-call(bf16[64,256,128]{2,1,0:T(8,128)(2,1)} %cot_hbm.1, bf16[64,256,128]{2,1,0:T(8,128)(2,1)} %pm_hbm.1, bf16[4096,256]{1,0:T(8,128)(2,1)} %constant.2.clone.sel_hbm, f32[64]{0:T(128)} %bias.1, ...), custom_call_target="tpu_custom_call" | custom-call | flops 7650410496 | bytes 16777216 | tf_op jit(solution)/shard_map/pallas_call | solution.py:549
  103.8 0.0 copy-start
  103.8 4.8 %copy.19 = bf16[64,256,128]{2,1,0:T(8,128)(2,1)} copy(bf16[64,256,128]{2,1,0:T(8,128)(2,1)} %get-tuple-element.16) | data formatting | bytes 8388608
  108.7 0.0 copy-done
  108.7 0.0 copy-start.1
  108.7 0.0 copy-start.2
  108.7 2.0 %copy.20 = bf16[64,256,128]{2,1,0:T(8,128)(2,1)} copy(bf16[64,256,128]{2,1,0:T(8,128)(2,1)S(1)} %copy-done) | data formatting | bytes 8388608
  110.7 0.0 copy-done.1
  110.7 0.7 copy.21
  111.4 0.0 copy-done.2
  111.4 0.6 copy.22
Async XLA Ops:
  103.8 4.9 %copy-start = (bf16[64,256,128]{2,1,0:T(8,128)(2,1)S(1)}, bf16[64,256,128]{2,1,0:T(8,128)(2,1)}, u32[]{:S(2)}) copy-start(bf16[64,256,128]{2,1,0:T(8,128)(2,1)} %get-tuple-element.17) | copy-start | bytes 12582916
  108.7 2.0 %copy-start.1 = (f32[9,64,64]{2,1,0:T(8,128)S(1)}, f32[9,64,64]{2,1,0:T(8,128)}, u32[]{:S(2)}) copy-start(f32[9,64,64]{2,1,0:T(8,128)} %get-tuple-element.10) | copy-start | bytes 442372
  108.7 2.7 %copy-start.2 = (f32[16,256]{1,0:T(8,128)S(1)}, f32[16,256]{1,0:T(8,128)}, u32[]{:S(2)}) copy-start(f32[16,256]{1,0:T(8,128)} %get-tuple-element.19) | copy-start | bytes 49156

commit v2 on v1

v2 whole, which is shorter than its diff:
```python
import functools
import math

import jax
import jax.numpy as jnp
from jax import lax
from jax.experimental import pallas as pl
from jax.experimental.pallas import tpu as pltpu
from jax.sharding import PartitionSpec as P

MESH = pl.DeviceIdType.MESH
BF = jnp.bfloat16
F32 = jnp.float32
NT = (((1,), (1,)), ((), ()))
PACK = 16
BLOCK = 32


def dot(a, b, dims=None):
    if dims is None:
        return jnp.dot(a, b, preferred_element_type=F32)
    return lax.dot_general(a, b, dims, preferred_element_type=F32)


def kernel(
    nr, nc, ch, ti, outer, comm, residues,
    cot_hbm, pm_hbm, bias, feat, lw, rw, ow, cw,
    po_hbm, pg_hbm, wg_out, fg_out,
    cot_n, hid_n, slope_n, wide, gt, cot_t, act_t, hx, even, odd, upd_even, upd_odd, packs, land_row, land_col,
    lr, left_in, right_in, left, left_t, mixf, mix, wf, wb, ow_q, mgf,
    wg_acc, wgs, land_a, land_b, fin, lg_acc, lg_out, rg_out, land_l, land_r,
    in_sem, out_sem, f_send, f_recv, h_send, h_recv, w_send, w_recv, g_send, g_recv,
):
    row = lax.axis_index("row")
    col = lax.axis_index("col")
    kg = ti // PACK
    ng = ti // 4
    pitch = ti + 8
    wch = ch + 8
    own = lr.shape[0]
    flat = row * nc + col
    goal = flat // nr
    slot = lax.rem(flat, nr)
    up, down = lax.rem(row + nr - 1, nr), lax.rem(row + 1, nr)
    west, east = lax.rem(col + nc - 1, nc), lax.rem(col + 1, nc)
    cstep = 8
    nchunk = ch // cstep

    cot_in = [
        pltpu.make_async_copy(
            cot_hbm.at[pl.ds(k * cstep, cstep)], cot_n.at[pl.ds(k * cstep, cstep)], in_sem.at[k]
        )
        for k in range(nchunk)
    ]
    pm_in = pltpu.make_async_copy(pm_hbm, hid_n, in_sem.at[nchunk])
    for copy in cot_in:
        copy.start()
    pm_in.start()

    def source(k):
        f = col * nr + k
        return f // nc, lax.rem(f, nc)

    if comm:
        barrier = pltpu.get_barrier_semaphore()

        def greet(r, c):
            pl.semaphore_signal(barrier, inc=1, device_id=(r, c), device_id_type=MESH)

        def greet_unless_me(r, c):
            @pl.when(jnp.logical_or(r != row, c != col))
            def _():
                greet(r, c)

        for d in range(1, nc):
            greet(row, lax.rem(col + d, nc))
        for d in range(1, nr):
            greet(lax.rem(row + d, nr), col)
        for r in (up, down):
            for c in (west, east):
                greet(r, c)
        for k in range(nr):
            greet_unless_me(k, goal)
            greet_unless_me(*source(k))
        total_greets = (nc - 1) + (nr - 1) + 4 + 2 * nr - jnp.where(goal == col, 2, 0)

    lr[...] = jnp.concatenate(
        [dot(feat[...], lw[...], NT), dot(feat[...], rw[...], NT), jnp.zeros((own, 128 - 2 * outer), F32)],
        axis=1,
    ).astype(BF)

    def remote(src, dst, ssem, rsem, dev):
        return pltpu.make_async_remote_copy(
            src_ref=src, dst_ref=dst, send_sem=ssem, recv_sem=rsem, device_id=dev, device_id_type=MESH
        )

    for a in range(3):
        wf[a * ch : (a + 1) * ch, :] = jnp.concatenate([cw[3 * a + b] for b in range(3)], axis=1)
        wb[a * ch : (a + 1) * ch, :] = jnp.concatenate(
            [cw[3 * a + b].astype(F32).T for b in range(3)], axis=1
        ).astype(BF)
    ow_q[...] = jnp.concatenate([ow[p] for p in range(outer)], axis=1)

    def p_widen():
        for k in range(nchunk):
            cot_in[k].wait()

            @pl.loop(0, cstep, unroll=2)
            def _(c):
                at = pl.multiple_of((k * cstep + c) * pitch, 8)
                wide[pl.ds(at, ti), :] = cot_n[k * cstep + c].astype(F32)

    p_widen()

    left_in[col] = lr[...]
    left_moves, right_moves = [], []
    if comm:
        pl.semaphore_wait(barrier, total_greets)
        for d in range(1, nc):
            move = remote(
                lr, left_in.at[col], f_send.at[d], f_recv.at[d], (row, lax.rem(col + d, nc))
            )
            move.start()
            left_moves.append(move)
        for k in range(nr):
            me = jnp.logical_and(row == k, goal == col)
            far = remote(
                lr, right_in.at[slot], f_send.at[nc + k], f_recv.at[nc + slot], (k, goal)
            )
            near = pltpu.make_async_copy(lr, right_in.at[slot], f_recv.at[nc + slot])

            @pl.when(me)
            def _():
                near.start()

            @pl.when(jnp.logical_not(me))
            def _():
                far.start()

            right_moves.append((me, far))

    lane = lax.broadcasted_iota(jnp.int32, (ch, 128), 1)
    window = lax.rem(lane + 4, 128) // 8

    def to_rows(dst, first, which):
        @pl.loop(0, kg, unroll=2)
        def _(k):
            packed = None
            for m in range(PACK):
                row_at = PACK * k + m
                x = wide[pl.ds(row_at, ch, stride=pitch), :].astype(BF)
                dst[first + row_at] = x
                packed = x if m == 0 else jnp.where(window == m, pltpu.roll(x, 8 * m, 1), packed)
            packs[which, k] = packed

    def halo_moves(src, first, which):
        edges = packs.at[which]
        from_west, from_east = land_col.at[which, 0], land_col.at[which, 1]
        plan = [
            (src.at[pl.ds(first, 4)], land_row.at[which, 1], (up, col)),
            (src.at[pl.ds(first + ti - 4, 4)], land_row.at[which, 0], (down, col)),
            (edges, from_east.at[pl.ds(1, kg)], (row, west)),
            (edges, from_west.at[pl.ds(1, kg)], (row, east)),
            (edges.at[0], from_east.at[kg + 1], (up, west)),
            (edges.at[0], from_west.at[kg + 1], (up, east)),
            (edges.at[kg - 1], from_east.at[0], (down, west)),
            (edges.at[kg - 1], from_west.at[0], (down, east)),
        ]
        return [
            remote(s, d, h_send.at[which, m], h_recv.at[which, m], dev)
            for m, (s, d, dev) in enumerate(plan)
        ]

    to_rows(cot_t, 4, 0)
    cot_moves = halo_moves(cot_t, 4, 0)
    if comm:
        for move in cot_moves:
            move.start()

    if comm:
        for d in range(1, nc):
            left_moves[d - 1].wait_recv()
        for k in range(nr):
            pltpu.make_async_copy(lr, right_in.at[k], f_recv.at[nc + k]).wait()
    left[...] = left_in[...].reshape(nc * own, 128)[:, :outer]
    left_t[...] = left[...].astype(F32).T.astype(BF)
    right = right_in[...].reshape(nr * own, 128)[:, outer : 2 * outer]
    step = 512
    for s in range(outer * ch // step):
        w = ow_q[:, s * step : (s + 1) * step].astype(F32).T.astype(BF)
        rows = dot(w, right, NT).astype(BF).astype(F32)
        for m in range(step // ch):
            at = (s * (step // ch) + m) * wch
            mixf[at : at + ch, :] = rows[m * ch : (m + 1) * ch]

    @pl.loop(0, ch, unroll=4)
    def _(c):
        mix[c] = mixf[pl.ds(c, outer, stride=wch), :].astype(BF)

    pm_in.wait()

    def p_hidden():
        def update(c):
            return dot(left[...], jnp.concatenate([mix[c], mix[c + 1]], axis=1))

        def finish(c, change):
            for k in range(2):
                hidden = (hid_n[c + k].astype(F32) + change[:, 128 * k : 128 * (k + 1)]).astype(BF)
                hid_n[c + k] = hidden
                h = hidden.astype(F32)
                e = jnp.exp(jnp.minimum(h, 0.0))
                slope_n[c + k] = e.astype(BF)
                at = pl.multiple_of((c + k) * pitch, 8)
                wide[pl.ds(at, ti), :] = jnp.where(h > 0, h, e - 1.0)

        upd_even[...] = update(0)

        @pl.loop(0, ch, step=4)
        def _(c):
            upd_odd[...] = update(c + 2)
            finish(c, upd_even[...])
            upd_even[...] = update(jnp.minimum(c + 4, ch - 2))
            finish(c + 2, upd_odd[...])

    p_hidden()

    to_rows(act_t, 8, 1)
    for s in (0, 4, ti + 8, ti + 12):
        act_t[s : s + 4] = jnp.zeros((4, ch, 128), BF)
    act_moves = halo_moves(act_t, 8, 1)
    if comm:
        for move in act_moves:
            move.start()

    has_up, has_down, has_west, has_east = row > 0, row < nr - 1, col > 0, col < nc - 1

    def keep(ok, x):
        return jnp.where(ok, x, jnp.zeros_like(x))

    def unpack_edges(dst, first, which):
        dst[first : first + 4] = keep(has_up, land_row[which, 0])
        dst[first + ti + 4 : first + ti + 8] = keep(has_down, land_row[which, 1])

        def place(k, ok):
            from_west = keep(jnp.logical_and(ok, has_west), land_col[which, 0, k])
            from_east = keep(jnp.logical_and(ok, has_east), land_col[which, 1, k])
            hx[k] = jnp.where(
                lax.rem(lane, 8) < 4, pltpu.roll(from_west, 4, 1), pltpu.roll(from_east, 124, 1)
            )

        place(0, has_up)
        place(kg + 1, has_down)

        @pl.loop(1, kg + 1, unroll=4)
        def _(k):
            place(k, True)

    def fill(dst, src, first, n, q, turned):
        for r in range(8):
            x = src[first + 16 * n + q + r]
            at = q + r + PACK - 4
            edge = pltpu.roll(hx[n + at // PACK], (PACK - at % PACK) % PACK * 8, 1)
            before = jnp.where(lane < 4, edge, pltpu.roll(x, 4, 1))
            after = jnp.where(lane >= 124, edge, pltpu.roll(x, 124, 1))
            lanes = slice(128 * r, 128 * (r + 1))
            dst[:ch, lanes] = after if turned else before
            dst[ch : 2 * ch, lanes] = x
            dst[2 * ch :, lanes] = before if turned else after

    def halves(x):
        return [x[:, :512], x[:, 512:]]

    def spread(parts, g, order):
        for s in range(len(parts) + 2):
            terms = [
                parts[s - k][a * ch : (a + 1) * ch]
                for k, a in enumerate(order)
                if 0 <= s - k < len(parts)
            ]
            total = terms[0]
            for term in terms[1:]:
                total = total + term
            for r in range(4):
                at = pl.ds(pl.multiple_of((4 * (g + s) + r) * wch, 8), ch)
                term = total[:, 128 * r : 128 * (r + 1)]
                gt[at, :] = gt[at, :] + term if s < 2 else term

    if comm:
        for move in cot_moves:
            move.wait_recv()
    unpack_edges(cot_t, 0, 0)
    gt[: 8 * wch] = jnp.zeros((8 * wch, 128), F32)
    wg_acc[...] = jnp.zeros_like(wg_acc)

    def p_back():
        fill(even, cot_t, 0, 0, 0, True)

        def acts(first):
            return jnp.concatenate(
                [
                    jnp.concatenate([act_t[first + 4 * a + r] for r in range(8)], axis=1)
                    for a in range(3)
                ],
                axis=0,
            )

        @pl.loop(0, ti // 16)
        def _(n):
            parts = halves(dot(wb[...], even[...]))
            grad = dot(even[...], acts(16 * n), NT)
            fill(odd, cot_t, 0, n, 8, True)
            parts += halves(dot(wb[...], odd[...]))
            grad = grad + dot(odd[...], acts(16 * n + 8), NT)
            fill(even, cot_t, 0, n, 16, True)
            spread(parts, 4 * n, (0, 1, 2))
            wg_acc[...] += grad

        spread(halves(dot(wb[...], even[...])), ng, (0, 1, 2))
        wg_acc[...] += dot(even[...], acts(ti), NT)

    p_back()

    part = 2 * 3 * ch // nc
    wgs[: 3 * ch] = wg_acc[:, :128]
    wgs[3 * ch :] = jnp.concatenate([wg_acc[:, 128:], jnp.zeros((3 * ch, 256 - 3 * ch), F32)], axis=1)
    land_a[col] = wgs[pl.ds(pl.multiple_of(col * part, 8), part)]
    a_moves, b_moves, c_moves, l_moves, r_moves = [], [], [], [], []
    if comm:
        for d in range(1, nc):
            other = lax.rem(col + d, nc)
            move = remote(
                wgs.at[pl.ds(pl.multiple_of(other * part, 8), part)],
                land_a.at[col], w_send.at[d], w_recv.at[d], (row, other),
            )
            move.start()
            a_moves.append(move)

    pg_out = [
        pltpu.make_async_copy(
            cot_n.at[pl.ds(k * cstep, cstep)], pg_hbm.at[pl.ds(k * cstep, cstep)], out_sem.at[k]
        )
        for k in range(nchunk)
    ]
    lg_acc[...] = jnp.zeros_like(lg_acc)

    def p_grad(k):
        @pl.loop(k * cstep, (k + 1) * cstep, step=4)
        def _(c):
            grads = []
            for m in range(4):
                g = gt[pl.ds(8 * wch + c + m, ti, stride=wch), :]
                pg = (cot_n[c + m].astype(F32) + g * slope_n[c + m].astype(F32)).astype(BF)
                cot_n[c + m] = pg
                grads.append(pg)
            grads = jnp.concatenate(grads, axis=1)
            mixes = jnp.concatenate([mix[c + m] for m in range(4)], axis=1)
            lg_acc[...] += dot(mixes, grads, NT)
            mg = dot(left_t[...], grads)
            for m in range(4):
                mgf[pl.ds(c + m, outer, stride=wch), :] = mg[:, 128 * m : 128 * (m + 1)]

    for k in range(nchunk):
        p_grad(k)
        pg_out[k].start()

    mg = jnp.concatenate([mgf[p * wch : p * wch + ch, :] for p in range(outer)], axis=0)
    mg_hi = mg.astype(BF)
    mg_lo = (mg - mg_hi.astype(F32)).astype(BF)
    rg = (dot(ow_q[...], mg_hi) + dot(ow_q[...], mg_lo)).T
    rg_out[...] = rg.reshape(nr, own, outer)
    lg_out[...] = lg_acc[...].T.reshape(nc, own, outer)
    land_l[col] = lg_out[col]
    if comm:
        for d in range(1, nc):
            other = lax.rem(col + d, nc)
            move = remote(lg_out.at[other], land_l.at[col], g_send.at[d], g_recv.at[d], (row, other))
            move.start()
            l_moves.append(move)
        for k in range(nr):
            r, c = source(k)
            me = jnp.logical_and(r == row, c == col)
            far = remote(
                rg_out.at[k], land_r.at[row], g_send.at[nc + k], g_recv.at[nc + row], (r, c)
            )
            near = pltpu.make_async_copy(rg_out.at[k], land_r.at[row], g_recv.at[nc + row])

            @pl.when(me)
            def _():
                near.start()

            @pl.when(jnp.logical_not(me))
            def _():
                far.start()

            r_moves.append((me, far))
        for move in a_moves:
            move.wait_recv()
    total = land_a[0]
    for k in range(1, nc):
        total = total + land_a[k]
    land_b[row] = total
    if comm:
        for d in range(1, nr):
            move = remote(
                land_b.at[row], land_b.at[row], w_send.at[nc + d], w_recv.at[nc + d],
                (lax.rem(row + d, nr), col),
            )
            move.start()
            b_moves.append(move)
        for move in act_moves:
            move.wait_recv()
    unpack_edges(act_t, 4, 1)
    gt[: 8 * wch] = jnp.zeros((8 * wch, 128), F32)

    nblock = ti // BLOCK
    po_out = [
        pltpu.make_async_copy(
            hid_n.at[:, pl.ds(BLOCK * k, BLOCK)], po_hbm.at[:, pl.ds(BLOCK * k, BLOCK)],
            out_sem.at[nchunk + k],
        )
        for k in range(nblock)
    ]

    fill(even, act_t, 4, 0, 0, False)

    def p_forward(first, last):
        @pl.loop(first, last)
        def _(n):
            parts = halves(dot(wf[...], even[...]))
            fill(odd, act_t, 4, n, 8, False)
            parts += halves(dot(wf[...], odd[...]))
            fill(even, act_t, 4, n, 16, False)
            spread(parts, 4 * n, (2, 1, 0))

    def p_finish(k):
        @pl.loop(0, ch, unroll=16)
        def _(c):
            conv = gt[pl.ds((8 + BLOCK * k) * wch + c, BLOCK, stride=wch), :]
            h = hid_n[c, pl.ds(BLOCK * k, BLOCK), :].astype(F32)
            hid_n[c, pl.ds(BLOCK * k, BLOCK), :] = (h + bias[c] + conv).astype(BF)

    for k in range(nblock):
        p_forward(2 * k + 1 if k else 0, min(2 * k + 3, ti // 16))
        if k == nblock - 1:
            spread(halves(dot(wf[...], even[...])), ng, (2, 1, 0))
        p_finish(k)
        po_out[k].start()
        if k == nblock // 2 - 1:
            if comm:
                for move in b_moves:
                    move.wait_recv()
            total = land_b[0]
            for m in range(1, nr):
                total = total + land_b[m]
            fin[col] = total * (1.0 / residues)
            if comm:
                for d in range(1, nc):
                    move = remote(
                        fin.at[col], fin.at[col], w_send.at[nc + nr + d], w_recv.at[nc + nr + d],
                        (row, lax.rem(col + d, nc)),
                    )
                    move.start()
                    c_moves.append(move)

    if comm:
        for move in l_moves:
            move.wait_recv()
        for k in range(nr):
            pltpu.make_async_copy(rg_out.at[k], land_r.at[k], g_recv.at[nc + k]).wait()
    lg = land_l[0]
    for k in range(1, nc):
        lg = lg + land_l[k]
    rg = land_r[0]
    for k in range(1, nr):
        rg = rg + land_r[k]

    def exact(x, w):
        total = jnp.zeros((own, w.shape[1]), F32)
        for _ in range(3):
            head = x.astype(BF)
            total = total + dot(head, w)
            x = x - head.astype(F32)
        return total

    fg_out[...] = (exact(lg, lw[...]) + exact(rg, rw[...])) * (1.0 / math.sqrt(residues))

    if comm:
        for move in c_moves:
            move.wait_recv()
    whole = fin[...].reshape(6 * ch, 128)
    for a in range(3):
        for b in range(3):
            base = 3 * ch * (a // 2) + b * ch
            at = ch * (a % 2)
            wg_out[3 * a + b] = whole[base : base + ch, at : at + ch]

    for copy in pg_out + po_out:
        copy.wait()
    if comm:
        for move in left_moves + cot_moves + act_moves + a_moves + b_moves + c_moves + l_moves:
            move.wait_send()
        for me, far in right_moves + r_moves:

            @pl.when(jnp.logical_not(me))
            def _():
                far.wait_send()


def call(nr, nc, residues, comm, pair_map, features, lw, rw, ow, cw, bias, cot):
    ch, ti, tj = pair_map.shape
    own, feat = features.shape
    outer = lw.shape[1]
    kg = ti // PACK
    part = 6 * ch // nc
    any_spec = pl.BlockSpec(memory_space=pl.ANY)
    vmem = pl.BlockSpec(memory_space=pltpu.VMEM)
    smem = pl.BlockSpec(memory_space=pltpu.SMEM)
    V = pltpu.VMEM
    dma = pltpu.SemaphoreType.DMA
    scratch = [
        V((ch, ti, tj), BF),
        V((ch, ti, tj), BF),
        V((ch, ti, tj), BF),
        V((ch * (ti + 8), 128), F32),
        V(((ti + 20) * (ch + 8), 128), F32),
        V((ti + 8, ch, 128), BF),
        V((ti + 16, ch, 128), BF),
        V((kg + 2, ch, 128), BF),
        V((3 * ch, 1024), BF),
        V((3 * ch, 1024), BF),
        V((ti, 256), F32),
        V((ti, 256), F32),
        V((2, kg, ch, 128), BF),
        V((2, 2, 4, ch, 128), BF),
        V((2, 2, kg + 2, ch, 128), BF),
        V((own, 128), BF),
        V((nc, own, 128), BF),
        V((nr, own, 128), BF),
        V((ti, outer), BF),
        V((outer, ti), BF),
        V((outer * (ch + 8), 128), F32),
        V((ch, outer, 128), BF),
        V((3 * ch, 3 * ch), BF),
        V((3 * ch, 3 * ch), BF),
        V((outer, outer * ch), BF),
        V((outer * (ch + 8), 128), F32),
        V((3 * ch, 3 * ch), F32),
        V((6 * ch, 128), F32),
        V((nc, part, 128), F32),
        V((nr, part, 128), F32),
        V((nc, part, 128), F32),
        V((outer, ti), F32),
        V((nc, own, outer), F32),
        V((nr, own, outer), F32),
        V((nc, own, outer), F32),
        V((nr, own, outer), F32),
        dma((ch // 8 + 1,)),
        dma((ch // 8 + ti // BLOCK,)),
        dma((nc + nr,)),
        dma((nc + nr,)),
        dma((2, 8)),
        dma((2, 8)),
        dma((2 * nc + nr,)),
        dma((2 * nc + nr,)),
        dma((nc + nr,)),
        dma((nc + nr,)),
    ]
    macs = ti * tj * (27 * ch * ch + 3 * outer * ch)
    out = pl.pallas_call(
        functools.partial(kernel, nr, nc, ch, ti, outer, comm, residues),
        out_shape=[
            jax.ShapeDtypeStruct((ch, ti, tj), BF),
            jax.ShapeDtypeStruct((ch, ti, tj), BF),
            jax.ShapeDtypeStruct((9, ch, ch), F32),
            jax.ShapeDtypeStruct((own, feat), F32),
        ],
        in_specs=[any_spec, any_spec, smem] + [vmem] * 5,
        out_specs=[any_spec, any_spec, vmem, vmem],
        scratch_shapes=scratch,
        compiler_params=pltpu.CompilerParams(
            collective_id=0 if comm else None,
            has_side_effects=True,
            vmem_limit_bytes=60 * 1024 * 1024,
        ),
        cost_estimate=pl.CostEstimate(
            flops=2 * macs, bytes_accessed=8 * ch * ti * tj, transcendentals=2 * ch * ti * tj
        ),
    )(cot, pair_map, bias, features, lw.T, rw.T, ow, cw.reshape(9, ch, ch))
    return out[0], out[1], out[2].reshape(3, 3, ch, ch), out[3]


def solution(mesh):
    nr, nc = mesh.shape["row"], mesh.shape["col"]

    def shards(pair_map, features, lw, rw, ow, cw, bias, cot):
        return call(
            nr, nc, pair_map.shape[1] * nr, True, pair_map, features, lw, rw, ow, cw, bias, cot
        )

    in_specs = (
        P(None, "row", "col"),
        P(("row", "col"), None),
        P(),
        P(),
        P(),
        P(),
        P(),
        P(None, "row", "col"),
    )
    out_specs = (P(None, "row", "col"), P(None, "row", "col"), P(), P(("row", "col"), None))
    return jax.shard_map(shards, mesh=mesh, in_specs=in_specs, out_specs=out_specs, check_vma=False)
```

time: 112 us -> 63 us (0.56)
  Pallas kernels: 100 us -> 54 us
  local copies, waits for them, and re-layouts: 11.1 us -> 8.19 us
    pallas_call x1, Pallas kernels: 100 us -> 54 us  [call(): pl.pallas_call(functools.partial(kernel, nr, nc, ch, ti, outer, comm, res...]
    unnamed x12 -> x10, local copies, waits for them, and re-layouts: 11.1 us -> 8.19 us
where the time goes in v2:
time: 63 us; the launch traced here: 62.9 us
  Pallas kernels  54 us (86%)
  local copies, waits for them, and re-layouts  8.19 us (13%)
  between operations  0.65 us (1%)
    pallas_call x1, Pallas kernels, call(): pl.pallas_call(functools.partial(kernel, nr, nc, ch, ti, outer, comm, res...  54 us
    unnamed x10, local copies, waits for them, and re-layouts  8.19 us

profile of v2, /device:TPU:0, one launch (start us, length us, event | category | flops | bytes accessed | tf_op | source)
XLA Modules:
  0.0 62.9 jit_solution(17617399124959061141)
XLA Ops:
  0.6 54.0 %shard_map.111 = (bf16[64,256,128]{2,1,0:T(8,128)(2,1)}, bf16[64,256,128]{2,1,0:T(8,128)(2,1)}, f32[9,64,64]{2,1,0:T(8,128)}, f32[16,256]{1,0:T(8,128)}) custom-call(bf16[64,256,128]{2,1,0:T(8,128)(2,1)} %cot_hbm.1, bf16[64,256,128]{2,1,0:T(8,128)(2,1)} %pm_hbm.1, f32[64]{0:T(128)} %bias.1, bf16[16,256]{1,0:T(8,128)(2,1)} %feat.1, bf16[32,256]{1,0:T(8,128)(2,1)} %bitcast.6, ...), custom_call_target="tpu_custom_call" | custom-call | flops 7650410496 | bytes 16777216 | tf_op jit(solution)/shard_map/pallas_call | solution.py:569
  54.7 0.0 copy-start
  54.7 4.8 %copy.16 = bf16[64,256,128]{2,1,0:T(8,128)(2,1)} copy(bf16[64,256,128]{2,1,0:T(8,128)(2,1)} %get-tuple-element.16) | data formatting | bytes 8388608
  59.5 0.0 copy-done
  59.5 0.0 copy-start.1
  59.5 0.0 copy-start.2
  59.5 2.0 %copy.17 = bf16[64,256,128]{2,1,0:T(8,128)(2,1)} copy(bf16[64,256,128]{2,1,0:T(8,128)(2,1)S(1)} %copy-done) | data formatting | bytes 8388608
  61.6 0.0 copy-done.1
  61.6 0.7 %copy.18 = f32[3,3,64,64]{3,2,1,0:T(8,128)} copy(f32[3,3,64,64]{3,2,1,0:T(8,128)S(1)} %bitcast.4) | data formatting | bytes 294912
  62.3 0.0 copy-done.2
  62.3 0.6 copy.19
Async XLA Ops:
  54.7 4.9 %copy-start = (bf16[64,256,128]{2,1,0:T(8,128)(2,1)S(1)}, bf16[64,256,128]{2,1,0:T(8,128)(2,1)}, u32[]{:S(2)}) copy-start(bf16[64,256,128]{2,1,0:T(8,128)(2,1)} %get-tuple-element.17) | copy-start | bytes 12582916
  59.5 2.0 %copy-start.1 = (f32[9,64,64]{2,1,0:T(8,128)S(1)}, f32[9,64,64]{2,1,0:T(8,128)}, u32[]{:S(2)}) copy-start(f32[9,64,64]{2,1,0:T(8,128)} %get-tuple-element.10) | copy-start | bytes 442372
  59.5 2.7 %copy-start.2 = (f32[16,256]{1,0:T(8,128)S(1)}, f32[16,256]{1,0:T(8,128)}, u32[]{:S(2)}) copy-start(f32[16,256]{1,0:T(8,128)} %get-tuple-element.19) | copy-start | bytes 49156

commit v3 on v2

--- a/solution.py
+++ b/solution.py
@@ -14,6 +14,7 @@
 NT = (((1,), (1,)), ((), ()))
 PACK = 16
 BLOCK = 32
+STEP = 4
 
 
 def dot(a, b, dims=None):
@@ -24,12 +25,12 @@
 
 def kernel(
     nr, nc, ch, ti, outer, comm, residues,
-    cot_hbm, pm_hbm, bias, feat, lw, rw, ow, cw,
-    po_hbm, pg_hbm, wg_out, fg_out,
-    cot_n, hid_n, slope_n, wide, gt, cot_t, act_t, hx, even, odd, upd_even, upd_odd, packs, land_row, land_col,
+    cot_hbm, pm_hbm, feat, lw, rw, ow, cw,
+    hid_n, cot_n, gt, wg_out, fg_out,
+    slope_n, wide, cot_t, act_t, hx, even, odd, upd_even, upd_odd, packs, land_row, land_col,
     lr, left_in, right_in, left, left_t, mixf, mix, wf, wb, ow_q, mgf,
     wg_acc, wgs, land_a, land_b, fin, lg_acc, lg_out, rg_out, land_l, land_r,
-    in_sem, out_sem, f_send, f_recv, h_send, h_recv, w_send, w_recv, g_send, g_recv,
+    in_sem, f_send, f_recv, h_send, h_recv, w_send, w_recv, g_send, g_recv,
 ):
     row = lax.axis_index("row")
     col = lax.axis_index("col")
@@ -208,10 +209,10 @@
                 hidden = (hid_n[c + k].astype(F32) + change[:, 128 * k : 128 * (k + 1)]).astype(BF)
                 hid_n[c + k] = hidden
                 h = hidden.astype(F32)
-                e = jnp.exp(jnp.minimum(h, 0.0))
+                e = jnp.minimum(jnp.exp(h), 1.0)
                 slope_n[c + k] = e.astype(BF)
                 at = pl.multiple_of((c + k) * pitch, 8)
-                wide[pl.ds(at, ti), :] = jnp.where(h > 0, h, e - 1.0)
+                wide[pl.ds(at, ti), :] = jnp.maximum(h, e - 1.0)
 
         upd_even[...] = update(0)
 
@@ -304,14 +305,16 @@
                 axis=0,
             )
 
-        @pl.loop(0, ti // 16)
+        @pl.loop(0, ti // 16, step=STEP)
         def _(n):
-            parts = halves(dot(wb[...], even[...]))
-            grad = dot(even[...], acts(16 * n), NT)
-            fill(odd, cot_t, 0, n, 8, True)
-            parts += halves(dot(wb[...], odd[...]))
-            grad = grad + dot(odd[...], acts(16 * n + 8), NT)
-            fill(even, cot_t, 0, n, 16, True)
+            parts, grad = [], 0
+            for m in range(STEP):
+                parts += halves(dot(wb[...], even[...]))
+                grad = grad + dot(even[...], acts(16 * (n + m)), NT)
+                fill(odd, cot_t, 0, n + m, 8, True)
+                parts += halves(dot(wb[...], odd[...]))
+                grad = grad + dot(odd[...], acts(16 * (n + m) + 8), NT)
+                fill(even, cot_t, 0, n + m, 16, True)
             spread(parts, 4 * n, (0, 1, 2))
             wg_acc[...] += grad
 
@@ -335,33 +338,28 @@
             move.start()
             a_moves.append(move)
 
-    pg_out = [
-        pltpu.make_async_copy(
-            cot_n.at[pl.ds(k * cstep, cstep)], pg_hbm.at[pl.ds(k * cstep, cstep)], out_sem.at[k]
-        )
-        for k in range(nchunk)
-    ]
     lg_acc[...] = jnp.zeros_like(lg_acc)
 
-    def p_grad(k):
-        @pl.loop(k * cstep, (k + 1) * cstep, step=4)
+    def p_grad():
+        @pl.loop(0, ch, step=8)
         def _(c):
-            grads = []
-            for m in range(4):
-                g = gt[pl.ds(8 * wch + c + m, ti, stride=wch), :]
-                pg = (cot_n[c + m].astype(F32) + g * slope_n[c + m].astype(F32)).astype(BF)
-                cot_n[c + m] = pg
-                grads.append(pg)
-            grads = jnp.concatenate(grads, axis=1)
-            mixes = jnp.concatenate([mix[c + m] for m in range(4)], axis=1)
-            lg_acc[...] += dot(mixes, grads, NT)
-            mg = dot(left_t[...], grads)
-            for m in range(4):
-                mgf[pl.ds(c + m, outer, stride=wch), :] = mg[:, 128 * m : 128 * (m + 1)]
-
-    for k in range(nchunk):
-        p_grad(k)
-        pg_out[k].start()
+            lg = 0
+            for half in (c, c + 4):
+                grads = []
+                for m in range(4):
+                    g = gt[pl.ds(8 * wch + half + m, ti, stride=wch), :]
+                    pg = (cot_n[half + m].astype(F32) + g * slope_n[half + m].astype(F32)).astype(BF)
+                    cot_n[half + m] = pg
+                    grads.append(pg)
+                grads = jnp.concatenate(grads, axis=1)
+                mixes = jnp.concatenate([mix[half + m] for m in range(4)], axis=1)
+                lg = lg + dot(mixes, grads, NT)
+                mg = dot(left_t[...], grads)
+                for m in range(4):
+                    mgf[pl.ds(half + m, outer, stride=wch), :] = mg[:, 128 * m : 128 * (m + 1)]
+            lg_acc[...] += lg
+
+    p_grad()
 
     mg = jnp.concatenate([mgf[p * wch : p * wch + ch, :] for p in range(outer)], axis=0)
     mg_hi = mg.astype(BF)
@@ -412,55 +410,37 @@
     unpack_edges(act_t, 4, 1)
     gt[: 8 * wch] = jnp.zeros((8 * wch, 128), F32)
 
-    nblock = ti // BLOCK
-    po_out = [
-        pltpu.make_async_copy(
-            hid_n.at[:, pl.ds(BLOCK * k, BLOCK)], po_hbm.at[:, pl.ds(BLOCK * k, BLOCK)],
-            out_sem.at[nchunk + k],
-        )
-        for k in range(nblock)
-    ]
-
     fill(even, act_t, 4, 0, 0, False)
 
     def p_forward(first, last):
-        @pl.loop(first, last)
+        @pl.loop(first, last, step=STEP)
         def _(n):
-            parts = halves(dot(wf[...], even[...]))
-            fill(odd, act_t, 4, n, 8, False)
-            parts += halves(dot(wf[...], odd[...]))
-            fill(even, act_t, 4, n, 16, False)
+            parts = []
+            for m in range(STEP):
+                parts += halves(dot(wf[...], even[...]))
+                fill(odd, act_t, 4, n + m, 8, False)
+                parts += halves(dot(wf[...], odd[...]))
+                fill(even, act_t, 4, n + m, 16, False)
             spread(parts, 4 * n, (2, 1, 0))
 
-    def p_finish(k):
-        @pl.loop(0, ch, unroll=16)
-        def _(c):
-            conv = gt[pl.ds((8 + BLOCK * k) * wch + c, BLOCK, stride=wch), :]
-            h = hid_n[c, pl.ds(BLOCK * k, BLOCK), :].astype(F32)
-            hid_n[c, pl.ds(BLOCK * k, BLOCK), :] = (h + bias[c] + conv).astype(BF)
-
-    for k in range(nblock):
-        p_forward(2 * k + 1 if k else 0, min(2 * k + 3, ti // 16))
-        if k == nblock - 1:
-            spread(halves(dot(wf[...], even[...])), ng, (2, 1, 0))
-        p_finish(k)
-        po_out[k].start()
-        if k == nblock // 2 - 1:
-            if comm:
-                for move in b_moves:
-                    move.wait_recv()
-            total = land_b[0]
-            for m in range(1, nr):
-                total = total + land_b[m]
-            fin[col] = total * (1.0 / residues)
-            if comm:
-                for d in range(1, nc):
-                    move = remote(
-                        fin.at[col], fin.at[col], w_send.at[nc + nr + d], w_recv.at[nc + nr + d],
-                        (row, lax.rem(col + d, nc)),
-                    )
-                    move.start()
-                    c_moves.append(move)
+    p_forward(0, ti // 32)
+    if comm:
+        for move in b_moves:
+            move.wait_recv()
+    total = land_b[0]
+    for m in range(1, nr):
+        total = total + land_b[m]
+    fin[col] = total * (1.0 / residues)
+    if comm:
+        for d in range(1, nc):
+            move = remote(
+                fin.at[col], fin.at[col], w_send.at[nc + nr + d], w_recv.at[nc + nr + d],
+                (row, lax.rem(col + d, nc)),
+            )
+            move.start()
+            c_moves.append(move)
+    p_forward(ti // 32, ti // 16)
+    spread(halves(dot(wf[...], even[...])), ng, (2, 1, 0))
 
     if comm:
         for move in l_moves:
@@ -494,8 +474,6 @@
             at = ch * (a % 2)
             wg_out[3 * a + b] = whole[base : base + ch, at : at + ch]
 
-    for copy in pg_out + po_out:
-        copy.wait()
     if comm:
         for move in left_moves + cot_moves + act_moves + a_moves + b_moves + c_moves + l_moves:
             move.wait_send()
@@ -504,6 +482,40 @@
             @pl.when(jnp.logical_not(me))
             def _():
                 far.wait_send()
+
+
+def last_kernel(
+    hid_n, pg_n, gt, wg_in, fg_in, bias, po_hbm, pg_hbm, wg_hbm, fg_hbm, out_n, out_sem
+):
+    ch, ti, _ = hid_n.shape
+    wch = ch + 8
+    step = ch // 4
+    copies = [
+        pltpu.make_async_copy(
+            pg_n.at[pl.ds(k * step, step)], pg_hbm.at[pl.ds(k * step, step)], out_sem.at[k]
+        )
+        for k in range(4)
+    ]
+    copies.append(pltpu.make_async_copy(wg_in, wg_hbm, out_sem.at[4]))
+    copies.append(pltpu.make_async_copy(fg_in, fg_hbm, out_sem.at[5]))
+    for copy in copies:
+        copy.start()
+    for k in range(ti // BLOCK):
+
+        @pl.loop(0, ch, unroll=16)
+        def _(c):
+            conv = gt[pl.ds((8 + BLOCK * k) * wch + c, BLOCK, stride=wch), :]
+            h = hid_n[c, pl.ds(BLOCK * k, BLOCK), :].astype(F32)
+            out_n[c, pl.ds(BLOCK * k, BLOCK), :] = (h + bias[c] + conv).astype(BF)
+
+        copy = pltpu.make_async_copy(
+            out_n.at[:, pl.ds(BLOCK * k, BLOCK)], po_hbm.at[:, pl.ds(BLOCK * k, BLOCK)],
+            out_sem.at[6 + k],
+        )
+        copy.start()
+        copies.append(copy)
+    for copy in copies:
+        copy.wait()
 
 
 def call(nr, nc, residues, comm, pair_map, features, lw, rw, ow, cw, bias, cot):
@@ -519,10 +531,7 @@
     dma = pltpu.SemaphoreType.DMA
     scratch = [
         V((ch, ti, tj), BF),
-        V((ch, ti, tj), BF),
-        V((ch, ti, tj), BF),
         V((ch * (ti + 8), 128), F32),
-        V(((ti + 20) * (ch + 8), 128), F32),
         V((ti + 8, ch, 128), BF),
         V((ti + 16, ch, 128), BF),
         V((kg + 2, ch, 128), BF),
@@ -555,7 +564,6 @@
         V((nc, own, outer), F32),
         V((nr, own, outer), F32),
         dma((ch // 8 + 1,)),
-        dma((ch // 8 + ti // BLOCK,)),
         dma((nc + nr,)),
         dma((nc + nr,)),
         dma((2, 8)),
@@ -569,24 +577,42 @@
     out = pl.pallas_call(
         functools.partial(kernel, nr, nc, ch, ti, outer, comm, residues),
         out_shape=[
+            V((ch, ti, tj), BF),
+            V((ch, ti, tj), BF),
+            V(((ti + 20) * (ch + 8), 128), F32),
+            V((9, ch, ch), F32),
+            V((own, feat), F32),
+        ],
+        in_specs=[any_spec, any_spec] + [vmem] * 5,
+        out_specs=[vmem] * 5,
+        scratch_shapes=scratch,
+        compiler_params=pltpu.CompilerParams(
+            collective_id=0 if comm else None,
+            has_side_effects=True,
+            vmem_limit_bytes=40 * 1024 * 1024,
+        ),
+        cost_estimate=pl.CostEstimate(
+            flops=2 * macs, bytes_accessed=8 * ch * ti * tj, transcendentals=2 * ch * ti * tj
+        ),
+    )(cot, pair_map, features, lw.T, rw.T, ow, cw.reshape(9, ch, ch))
+    kept = [pltpu.with_memory_space_constraint(x, pltpu.VMEM) for x in out]
+    po, pg, wg, fg = pl.pallas_call(
+        last_kernel,
+        out_shape=[
             jax.ShapeDtypeStruct((ch, ti, tj), BF),
             jax.ShapeDtypeStruct((ch, ti, tj), BF),
             jax.ShapeDtypeStruct((9, ch, ch), F32),
             jax.ShapeDtypeStruct((own, feat), F32),
         ],
-        in_specs=[any_spec, any_spec, smem] + [vmem] * 5,
-        out_specs=[any_spec, any_spec, vmem, vmem],
-        scratch_shapes=scratch,
-        compiler_params=pltpu.CompilerParams(
-            collective_id=0 if comm else None,
-            has_side_effects=True,
-            vmem_limit_bytes=60 * 1024 * 1024,
+        in_specs=[vmem] * 5 + [smem],
+        out_specs=[any_spec] * 4,
+        scratch_shapes=[V((ch, ti, tj), BF), dma((6 + ti // BLOCK,))],
+        compiler_params=pltpu.CompilerParams(vmem_limit_bytes=24 * 1024 * 1024),
+        cost_estimate=pl.CostEstimate(
+            flops=2 * ch * ti * tj, bytes_accessed=4 * ch * ti * tj, transcendentals=0
         ),
-        cost_estimate=pl.CostEstimate(
-            flops=2 * macs, bytes_accessed=8 * ch * ti * tj, transcendentals=2 * ch * ti * tj
-        ),
-    )(cot, pair_map, bias, features, lw.T, rw.T, ow, cw.reshape(9, ch, ch))
-    return out[0], out[1], out[2].reshape(3, 3, ch, ch), out[3]
+    )(*kept, bias)
+    return po, pg, wg.reshape(3, 3, ch, ch), fg
 
 
 def solution(mesh):

time: 63 us -> 53.3 us (0.85); the launches traced: 62.9 us -> 52.4 us
  local copies, waits for them, and re-layouts: 8.19 us -> 0.01 us
  Pallas kernels: 54 us -> 51.7 us
    unnamed x10 -> x2, local copies, waits for them, and re-layouts: 8.19 us -> 0.01 us
    pallas_call x1, Pallas kernels: 54 us -> 47.7 us  [call(): pl.pallas_call(functools.partial(kernel, nr, nc, ch, ti, outer, comm, res...]
    pallas_call x0 -> x1, Pallas kernels: none -> 4.03 us  [call(): pl.pallas_call(last_kernel, out_shape=[jax.ShapeDtypeStruct((ch, ti, tj),...]
where the time goes in v3:
time: 53.3 us; the launch traced here: 52.4 us
  Pallas kernels  51.7 us (97%)
  between operations  0.66 us (1%)
    pallas_call x1, Pallas kernels, call(): pl.pallas_call(functools.partial(kernel, nr, nc, ch, ti, outer, comm, res...  47.7 us
    pallas_call x1, Pallas kernels, call(): pl.pallas_call(last_kernel, out_shape=[jax.ShapeDtypeStruct((ch, ti, tj),...  4.03 us

profile of v3, /device:TPU:0, one launch (start us, length us, event | category | flops | bytes accessed | tf_op | source)
XLA Modules:
  0.0 52.4 jit_solution(8770359192109433209)
XLA Ops:
  0.6 0.0 copy-start
  0.6 47.7 %shard_map.111 = (bf16[64,256,128]{2,1,0:T(8,128)(2,1)S(1)}, bf16[64,256,128]{2,1,0:T(8,128)(2,1)S(1)}, f32[19872,128]{1,0:T(8,128)S(1)}, f32[9,64,64]{2,1,0:T(8,128)S(1)}, f32[16,256]{1,0:T(8,128)S(1)}) custom-call(bf16[64,256,128]{2,1,0:T(8,128)(2,1)} %cot_hbm.1, bf16[64,256,128]{2,1,0:T(8,128)(2,1)} %pm_hbm.1, bf16[16,256]{1,0:T(8,128)(2,1)} %feat.1, ...), custom_call_target="tpu_custom_call" | custom-call | flops 7650410496 | bytes 16777216 | tf_op jit(solution)/shard_map/pallas_call | solution.py:577
  48.3 0.0 copy-done
  48.4 4.0 %shard_map.112 = (bf16[64,256,128]{2,1,0:T(8,128)(2,1)}, bf16[64,256,128]{2,1,0:T(8,128)(2,1)}, f32[9,64,64]{2,1,0:T(8,128)}, f32[16,256]{1,0:T(8,128)}) custom-call(bf16[64,256,128]{2,1,0:T(8,128)(2,1)S(1)} %get-tuple-element.13.hid_n, bf16[64,256,128]{2,1,0:T(8,128)(2,1)S(1)} %get-tuple-element.14.pg_n, f32[19872,128]{1,0:T(8,128)S(1)} %get-tuple-element.15.gt, ...), custom_call_target="tpu_custom_call" | custom-call | flops 4194304 | bytes 8388608 | tf_op jit(solution)/shard_map/pallas_call | solution.py:599
Async XLA Ops:
  0.6 47.7 %copy-start = (f32[64]{0:T(128)S(1)}, f32[64]{0:T(128)}, u32[]{:S(2)}) copy-start(f32[64]{0:T(128)} %bias.1) | copy-start | bytes 772

commit v4 on v3

--- a/solution.py
+++ b/solution.py
@@ -27,8 +27,8 @@
     nr, nc, ch, ti, outer, comm, residues,
     cot_hbm, pm_hbm, feat, lw, rw, ow, cw,
     hid_n, cot_n, gt, wg_out, fg_out,
-    slope_n, wide, cot_t, act_t, hx, even, odd, upd_even, upd_odd, packs, land_row, land_col,
-    lr, left_in, right_in, left, left_t, mixf, mix, wf, wb, ow_q, mgf,
+    slope_n, wide, cot_t, act_t, hx, terms, even, odd, upd_even, upd_odd, packs, land_row, land_col,
+    lr, left_in, right_in, left, left_t, mixf, mix, wf, wb, ow_q, ow_t, mgf,
     wg_acc, wgs, land_a, land_b, fin, lg_acc, lg_out, rg_out, land_l, land_r,
     in_sem, f_send, f_recv, h_send, h_recv, w_send, w_recv, g_send, g_recv,
 ):
@@ -95,12 +95,42 @@
             src_ref=src, dst_ref=dst, send_sem=ssem, recv_sem=rsem, device_id=dev, device_id_type=MESH
         )
 
+    left_in[col] = lr[...]
+    left_moves, right_moves = [], []
+    if comm:
+        pl.semaphore_wait(barrier, total_greets)
+        for d in range(1, nc):
+            move = remote(
+                lr, left_in.at[col], f_send.at[d], f_recv.at[d], (row, lax.rem(col + d, nc))
+            )
+            move.start()
+            left_moves.append(move)
+        for k in range(nr):
+            me = jnp.logical_and(row == k, goal == col)
+            far = remote(
+                lr, right_in.at[slot], f_send.at[nc + k], f_recv.at[nc + slot], (k, goal)
+            )
+            near = pltpu.make_async_copy(lr, right_in.at[slot], f_recv.at[nc + slot])
+
+            @pl.when(me)
+            def _():
+                near.start()
+
+            @pl.when(jnp.logical_not(me))
+            def _():
+                far.start()
+
+            right_moves.append((me, far))
+
     for a in range(3):
         wf[a * ch : (a + 1) * ch, :] = jnp.concatenate([cw[3 * a + b] for b in range(3)], axis=1)
         wb[a * ch : (a + 1) * ch, :] = jnp.concatenate(
             [cw[3 * a + b].astype(F32).T for b in range(3)], axis=1
         ).astype(BF)
     ow_q[...] = jnp.concatenate([ow[p] for p in range(outer)], axis=1)
+    step = 512
+    for k in range(outer * ch // step):
+        ow_t[k * step : (k + 1) * step, :] = ow_q[:, k * step : (k + 1) * step].astype(F32).T.astype(BF)
 
     def p_widen():
         for k in range(nchunk):
@@ -113,43 +143,16 @@
 
     p_widen()
 
-    left_in[col] = lr[...]
-    left_moves, right_moves = [], []
-    if comm:
-        pl.semaphore_wait(barrier, total_greets)
-        for d in range(1, nc):
-            move = remote(
-                lr, left_in.at[col], f_send.at[d], f_recv.at[d], (row, lax.rem(col + d, nc))
-            )
-            move.start()
-            left_moves.append(move)
-        for k in range(nr):
-            me = jnp.logical_and(row == k, goal == col)
-            far = remote(
-                lr, right_in.at[slot], f_send.at[nc + k], f_recv.at[nc + slot], (k, goal)
-            )
-            near = pltpu.make_async_copy(lr, right_in.at[slot], f_recv.at[nc + slot])
-
-            @pl.when(me)
-            def _():
-                near.start()
-
-            @pl.when(jnp.logical_not(me))
-            def _():
-                far.start()
-
-            right_moves.append((me, far))
-
     lane = lax.broadcasted_iota(jnp.int32, (ch, 128), 1)
     window = lax.rem(lane + 4, 128) // 8
 
-    def to_rows(dst, first, which):
+    def to_rows(dst, first, which, read):
         @pl.loop(0, kg, unroll=2)
         def _(k):
             packed = None
             for m in range(PACK):
                 row_at = PACK * k + m
-                x = wide[pl.ds(row_at, ch, stride=pitch), :].astype(BF)
+                x = read(row_at).astype(BF)
                 dst[first + row_at] = x
                 packed = x if m == 0 else jnp.where(window == m, pltpu.roll(x, 8 * m, 1), packed)
             packs[which, k] = packed
@@ -172,7 +175,7 @@
             for m, (s, d, dev) in enumerate(plan)
         ]
 
-    to_rows(cot_t, 4, 0)
+    to_rows(cot_t, 4, 0, lambda i: wide[pl.ds(i, ch, stride=pitch), :])
     cot_moves = halo_moves(cot_t, 4, 0)
     if comm:
         for move in cot_moves:
@@ -186,15 +189,13 @@
     left[...] = left_in[...].reshape(nc * own, 128)[:, :outer]
     left_t[...] = left[...].astype(F32).T.astype(BF)
     right = right_in[...].reshape(nr * own, 128)[:, outer : 2 * outer]
-    step = 512
-    for s in range(outer * ch // step):
-        w = ow_q[:, s * step : (s + 1) * step].astype(F32).T.astype(BF)
-        rows = dot(w, right, NT).astype(BF).astype(F32)
+    for k in range(outer * ch // step):
+        rows = dot(ow_t[k * step : (k + 1) * step, :], right, NT).astype(BF).astype(F32)
         for m in range(step // ch):
-            at = (s * (step // ch) + m) * wch
+            at = (k * (step // ch) + m) * wch
             mixf[at : at + ch, :] = rows[m * ch : (m + 1) * ch]
 
-    @pl.loop(0, ch, unroll=4)
+    @pl.loop(0, ch, unroll=8)
     def _(c):
         mix[c] = mixf[pl.ds(c, outer, stride=wch), :].astype(BF)
 
@@ -211,8 +212,7 @@
                 h = hidden.astype(F32)
                 e = jnp.minimum(jnp.exp(h), 1.0)
                 slope_n[c + k] = e.astype(BF)
-                at = pl.multiple_of((c + k) * pitch, 8)
-                wide[pl.ds(at, ti), :] = jnp.maximum(h, e - 1.0)
+                wide[pl.ds(c + k, ti, stride=wch), :] = jnp.maximum(h, e - 1.0)
 
         upd_even[...] = update(0)
 
@@ -225,7 +225,7 @@
 
     p_hidden()
 
-    to_rows(act_t, 8, 1)
+    to_rows(act_t, 8, 1, lambda i: wide[pl.ds(pl.multiple_of(i * wch, 8), ch), :])
     for s in (0, 4, ti + 8, ti + 12):
         act_t[s : s + 4] = jnp.zeros((4, ch, 128), BF)
     act_moves = halo_moves(act_t, 8, 1)
@@ -293,8 +293,8 @@
     gt[: 8 * wch] = jnp.zeros((8 * wch, 128), F32)
     wg_acc[...] = jnp.zeros_like(wg_acc)
 
-    def p_back():
-        fill(even, cot_t, 0, 0, 0, True)
+    def p_kernel():
+        fill(terms.at[0], cot_t, 0, 0, 0, True)
 
         def acts(first):
             return jnp.concatenate(
@@ -307,21 +307,27 @@
 
         @pl.loop(0, ti // 16, step=STEP)
         def _(n):
-            parts, grad = [], 0
-            for m in range(STEP):
-                parts += halves(dot(wb[...], even[...]))
-                grad = grad + dot(even[...], acts(16 * (n + m)), NT)
-                fill(odd, cot_t, 0, n + m, 8, True)
-                parts += halves(dot(wb[...], odd[...]))
-                grad = grad + dot(odd[...], acts(16 * (n + m) + 8), NT)
-                fill(even, cot_t, 0, n + m, 16, True)
+            grad = 0
+            for m in range(n_chunks):
+                j = 2 * n + m
+                grad = grad + dot(terms[j], acts(8 * j), NT)
+                fill(terms.at[j + 1], cot_t, 0, n + (m + 1) // 2, 8 * ((m + 1) % 2), True)
+            wg_acc[...] += grad
+
+        wg_acc[...] += dot(terms[ti // 8], acts(ti), NT)
+
+    def p_back():
+        @pl.loop(0, ti // 16, step=STEP)
+        def _(n):
+            parts = []
+            for m in range(n_chunks):
+                parts += halves(dot(wb[...], terms[2 * n + m]))
             spread(parts, 4 * n, (0, 1, 2))
-            wg_acc[...] += grad
-
-        spread(halves(dot(wb[...], even[...])), ng, (0, 1, 2))
-        wg_acc[...] += dot(even[...], acts(ti), NT)
-
-    p_back()
+
+        spread(halves(dot(wb[...], terms[ti // 8])), ng, (0, 1, 2))
+
+    n_chunks = 2 * STEP
+    p_kernel()
 
     part = 2 * 3 * ch // nc
     wgs[: 3 * ch] = wg_acc[:, :128]
@@ -337,6 +343,24 @@
             )
             move.start()
             a_moves.append(move)
+
+    p_back()
+
+    if comm:
+        for move in a_moves:
+            move.wait_recv()
+    total = land_a[0]
+    for k in range(1, nc):
+        total = total + land_a[k]
+    land_b[row] = total
+    if comm:
+        for d in range(1, nr):
+            move = remote(
+                land_b.at[row], land_b.at[row], w_send.at[nc + d], w_recv.at[nc + d],
+                (lax.rem(row + d, nr), col),
+            )
+            move.start()
+            b_moves.append(move)
 
     lg_acc[...] = jnp.zeros_like(lg_acc)
 
@@ -391,20 +415,20 @@
                 far.start()
 
             r_moves.append((me, far))
-        for move in a_moves:
+        for move in b_moves:
             move.wait_recv()
-    total = land_a[0]
-    for k in range(1, nc):
-        total = total + land_a[k]
-    land_b[row] = total
-    if comm:
-        for d in range(1, nr):
+    total = land_b[0]
+    for m in range(1, nr):
+        total = total + land_b[m]
+    fin[col] = total * (1.0 / residues)
+    if comm:
+        for d in range(1, nc):
             move = remote(
-                land_b.at[row], land_b.at[row], w_send.at[nc + d], w_recv.at[nc + d],
-                (lax.rem(row + d, nr), col),
+                fin.at[col], fin.at[col], w_send.at[nc + nr + d], w_recv.at[nc + nr + d],
+                (row, lax.rem(col + d, nc)),
             )
             move.start()
-            b_moves.append(move)
+            c_moves.append(move)
         for move in act_moves:
             move.wait_recv()
     unpack_edges(act_t, 4, 1)
@@ -423,23 +447,7 @@
                 fill(even, act_t, 4, n + m, 16, False)
             spread(parts, 4 * n, (2, 1, 0))
 
-    p_forward(0, ti // 32)
-    if comm:
-        for move in b_moves:
-            move.wait_recv()
-    total = land_b[0]
-    for m in range(1, nr):
-        total = total + land_b[m]
-    fin[col] = total * (1.0 / residues)
-    if comm:
-        for d in range(1, nc):
-            move = remote(
-                fin.at[col], fin.at[col], w_send.at[nc + nr + d], w_recv.at[nc + nr + d],
-                (row, lax.rem(col + d, nc)),
-            )
-            move.start()
-            c_moves.append(move)
-    p_forward(ti // 32, ti // 16)
+    p_forward(0, ti // 16)
     spread(halves(dot(wf[...], even[...])), ng, (2, 1, 0))
 
     if comm:
@@ -531,10 +539,11 @@
     dma = pltpu.SemaphoreType.DMA
     scratch = [
         V((ch, ti, tj), BF),
-        V((ch * (ti + 8), 128), F32),
+        V((max(ch * (ti + 8), ti * (ch + 8)), 128), F32),
         V((ti + 8, ch, 128), BF),
         V((ti + 16, ch, 128), BF),
         V((kg + 2, ch, 128), BF),
+        V((ti // 8 + 1, 3 * ch, 1024), BF),
         V((3 * ch, 1024), BF),
         V((3 * ch, 1024), BF),
         V((ti, 256), F32),
@@ -552,6 +561,7 @@
         V((3 * ch, 3 * ch), BF),
         V((3 * ch, 3 * ch), BF),
         V((outer, outer * ch), BF),
+        V((outer * ch, outer), BF),
         V((outer * (ch + 8), 128), F32),
         V((3 * ch, 3 * ch), F32),
         V((6 * ch, 128), F32),
@@ -589,7 +599,7 @@
         compiler_params=pltpu.CompilerParams(
             collective_id=0 if comm else None,
             has_side_effects=True,
-            vmem_limit_bytes=40 * 1024 * 1024,
+            vmem_limit_bytes=44 * 1024 * 1024,
         ),
         cost_estimate=pl.CostEstimate(
             flops=2 * macs, bytes_accessed=8 * ch * ti * tj, transcendentals=2 * ch * ti * tj

time: 53.3 us -> 52.1 us (0.977)
  the two profiles are of different devices: /device:TPU:0 before, /device:TPU:3 now
where the time goes in v4:
time: 52.1 us; the launch traced here: 51.9 us
  Pallas kernels  51.3 us (98%)
  between operations  0.66 us (1%)
    pallas_call x1, Pallas kernels, call(): pl.pallas_call(functools.partial(kernel, nr, nc, ch, ti, outer, comm, res...  47.2 us
    pallas_call x1, Pallas kernels, call(): pl.pallas_call(last_kernel, out_shape=[jax.ShapeDtypeStruct((ch, ti, tj),...  4.03 us

profile of v4, /device:TPU:3, one launch (start us, length us, event | category | flops | bytes accessed | tf_op | source)
XLA Modules:
  0.0 51.9 jit_solution(8714790923894651707)
XLA Ops:
  0.6 0.0 copy-start
  0.6 47.2 %shard_map.111 = (bf16[64,256,128]{2,1,0:T(8,128)(2,1)S(1)}, bf16[64,256,128]{2,1,0:T(8,128)(2,1)S(1)}, f32[19872,128]{1,0:T(8,128)S(1)}, f32[9,64,64]{2,1,0:T(8,128)S(1)}, f32[16,256]{1,0:T(8,128)S(1)}) custom-call(bf16[64,256,128]{2,1,0:T(8,128)(2,1)} %cot_hbm.1, bf16[64,256,128]{2,1,0:T(8,128)(2,1)} %pm_hbm.1, bf16[16,256]{1,0:T(8,128)(2,1)} %feat.1, ...), custom_call_target="tpu_custom_call" | custom-call | flops 7650410496 | bytes 16777216 | tf_op jit(solution)/shard_map/pallas_call | solution.py:587
  47.9 0.0 copy-done
  47.9 4.0 %shard_map.112 = (bf16[64,256,128]{2,1,0:T(8,128)(2,1)}, bf16[64,256,128]{2,1,0:T(8,128)(2,1)}, f32[9,64,64]{2,1,0:T(8,128)}, f32[16,256]{1,0:T(8,128)}) custom-call(bf16[64,256,128]{2,1,0:T(8,128)(2,1)S(1)} %get-tuple-element.13.hid_n, bf16[64,256,128]{2,1,0:T(8,128)(2,1)S(1)} %get-tuple-element.14.pg_n, f32[19872,128]{1,0:T(8,128)S(1)} %get-tuple-element.15.gt, ...), custom_call_target="tpu_custom_call" | custom-call | flops 4194304 | bytes 8388608 | tf_op jit(solution)/shard_map/pallas_call | solution.py:609
Async XLA Ops:
  0.6 47.3 %copy-start = (f32[64]{0:T(128)S(1)}, f32[64]{0:T(128)}, u32[]{:S(2)}) copy-start(f32[64]{0:T(128)} %bias.1) | copy-start | bytes 772

commit v5 on v4

--- a/solution.py
+++ b/solution.py
@@ -329,38 +329,67 @@
     n_chunks = 2 * STEP
     p_kernel()
 
-    part = 2 * 3 * ch // nc
-    wgs[: 3 * ch] = wg_acc[:, :128]
-    wgs[3 * ch :] = jnp.concatenate([wg_acc[:, 128:], jnp.zeros((3 * ch, 256 - 3 * ch), F32)], axis=1)
-    land_a[col] = wgs[pl.ds(pl.multiple_of(col * part, 8), part)]
+    taps = 9
+    owners = [min(2 * k, nc - 1) for k in range(taps)]
+    is_owner = functools.reduce(jnp.logical_or, [col == c for c in owners])
+    mine = jnp.where(col == owners[-1], taps - 1, col // 2)
+    half = ch // 2
+    for k in range(taps):
+        a, b = k // 3, k % 3
+        tap = wg_acc[b * ch : (b + 1) * ch, a * ch : (a + 1) * ch]
+        wgs[k] = jnp.concatenate([tap[:half], tap[half:]], axis=1).astype(BF)
     a_moves, b_moves, c_moves, l_moves, r_moves = [], [], [], [], []
-    if comm:
-        for d in range(1, nc):
-            other = lax.rem(col + d, nc)
-            move = remote(
-                wgs.at[pl.ds(pl.multiple_of(other * part, 8), part)],
-                land_a.at[col], w_send.at[d], w_recv.at[d], (row, other),
-            )
-            move.start()
-            a_moves.append(move)
+    for k, c in enumerate(owners):
+        move = remote(wgs.at[k], land_a.at[col], w_send.at[k], w_recv.at[col], (row, c))
+
+        @pl.when(col == c)
+        def _():
+            land_a[col] = wgs[k]
+
+        if comm:
+
+            @pl.when(col != c)
+            def _():
+                move.start()
+
+            a_moves.append((c, move))
 
     p_back()
 
-    if comm:
-        for move in a_moves:
-            move.wait_recv()
-    total = land_a[0]
-    for k in range(1, nc):
-        total = total + land_a[k]
-    land_b[row] = total
-    if comm:
-        for d in range(1, nr):
-            move = remote(
-                land_b.at[row], land_b.at[row], w_send.at[nc + d], w_recv.at[nc + d],
+    def each(refs):
+        total = refs[0].astype(F32)
+        for k in range(1, refs.shape[0]):
+            total = total + refs[k].astype(F32)
+        return total
+
+    for d in range(1, nr):
+        b_moves.append(
+            remote(
+                land_b.at[row], land_b.at[row], w_send.at[taps + d], w_recv.at[nc + d],
                 (lax.rem(row + d, nr), col),
             )
-            move.start()
-            b_moves.append(move)
+        )
+    for d in range(1, nc):
+        c_moves.append(
+            remote(
+                fin.at[mine], fin.at[mine], w_send.at[taps + nr + d], w_recv.at[nc + nr + mine],
+                (row, lax.rem(col + d, nc)),
+            )
+        )
+
+    @pl.when(is_owner)
+    def _():
+        if comm:
+            for c in range(nc):
+
+                @pl.when(col != c)
+                def _():
+                    pltpu.make_async_copy(wgs.at[0], land_a.at[c], w_recv.at[c]).wait()
+
+        land_b[row] = each(land_a)
+        if comm:
+            for move in b_moves:
+                move.start()
 
     lg_acc[...] = jnp.zeros_like(lg_acc)
 
@@ -415,20 +444,18 @@
                 far.start()
 
             r_moves.append((me, far))
-        for move in b_moves:
-            move.wait_recv()
-    total = land_b[0]
-    for m in range(1, nr):
-        total = total + land_b[m]
-    fin[col] = total * (1.0 / residues)
-    if comm:
-        for d in range(1, nc):
-            move = remote(
-                fin.at[col], fin.at[col], w_send.at[nc + nr + d], w_recv.at[nc + nr + d],
-                (row, lax.rem(col + d, nc)),
-            )
-            move.start()
-            c_moves.append(move)
+
+    @pl.when(is_owner)
+    def _():
+        if comm:
+            for move in b_moves:
+                move.wait_recv()
+        fin[mine] = (each(land_b) * (1.0 / residues)).astype(BF)
+        if comm:
+            for move in c_moves:
+                move.start()
+
+    if comm:
         for move in act_moves:
             move.wait_recv()
     unpack_edges(act_t, 4, 1)
@@ -472,19 +499,30 @@
 
     fg_out[...] = (exact(lg, lw[...]) + exact(rg, rw[...])) * (1.0 / math.sqrt(residues))
 
-    if comm:
-        for move in c_moves:
-            move.wait_recv()
-    whole = fin[...].reshape(6 * ch, 128)
-    for a in range(3):
-        for b in range(3):
-            base = 3 * ch * (a // 2) + b * ch
-            at = ch * (a % 2)
-            wg_out[3 * a + b] = whole[base : base + ch, at : at + ch]
-
-    if comm:
-        for move in left_moves + cot_moves + act_moves + a_moves + b_moves + c_moves + l_moves:
+    for k, c in enumerate(owners):
+        if comm:
+
+            @pl.when(col != c)
+            def _():
+                pltpu.make_async_copy(wgs.at[0], fin.at[k], w_recv.at[nc + nr + k]).wait()
+
+        tap = fin[k].astype(F32)
+        wg_out[k] = jnp.concatenate([tap[:, :ch], tap[:, ch:]], axis=0)
+
+    if comm:
+        for move in left_moves + cot_moves + act_moves + l_moves:
             move.wait_send()
+        for c, move in a_moves:
+
+            @pl.when(col != c)
+            def _():
+                move.wait_send()
+
+        @pl.when(is_owner)
+        def _():
+            for move in b_moves + c_moves:
+                move.wait_send()
+
         for me, far in right_moves + r_moves:
 
             @pl.when(jnp.logical_not(me))
@@ -531,7 +569,6 @@
     own, feat = features.shape
     outer = lw.shape[1]
     kg = ti // PACK
-    part = 6 * ch // nc
     any_spec = pl.BlockSpec(memory_space=pl.ANY)
     vmem = pl.BlockSpec(memory_space=pltpu.VMEM)
     smem = pl.BlockSpec(memory_space=pltpu.SMEM)
@@ -564,10 +601,10 @@
         V((outer * ch, outer), BF),
         V((outer * (ch + 8), 128), F32),
         V((3 * ch, 3 * ch), F32),
-        V((6 * ch, 128), F32),
-        V((nc, part, 128), F32),
-        V((nr, part, 128), F32),
-        V((nc, part, 128), F32),
+        V((9, ch // 2, 2 * ch), BF),
+        V((nc, ch // 2, 2 * ch), BF),
+        V((nr, ch // 2, 2 * ch), F32),
+        V((9, ch // 2, 2 * ch), BF),
         V((outer, ti), F32),
         V((nc, own, outer), F32),
         V((nr, own, outer), F32),
@@ -578,8 +615,8 @@
         dma((nc + nr,)),
         dma((2, 8)),
         dma((2, 8)),
-        dma((2 * nc + nr,)),
-        dma((2 * nc + nr,)),
+        dma((9 + nr + nc,)),
+        dma((nc + nr + 9,)),
         dma((nc + nr,)),
         dma((nc + nr,)),
     ]

time: 52.1 us -> 50.6 us (0.971)
  the two profiles are of different devices: /device:TPU:3 before, /device:TPU:0 now
where the time goes in v5:
time: 50.6 us; the launch traced here: 50.4 us
  Pallas kernels  49.8 us (98%)
  between operations  0.66 us (1%)
    pallas_call x1, Pallas kernels, call(): pl.pallas_call(functools.partial(kernel, nr, nc, ch, ti, outer, comm, res...  45.7 us
    pallas_call x1, Pallas kernels, call(): pl.pallas_call(last_kernel, out_shape=[jax.ShapeDtypeStruct((ch, ti, tj),...  4.03 us

profile of v5, /device:TPU:0, one launch (start us, length us, event | category | flops | bytes accessed | tf_op | source)
XLA Modules:
  0.0 50.4 jit_solution(99907001995606759)
XLA Ops:
  0.6 0.0 copy-start
  0.6 45.7 %shard_map.111 = (bf16[64,256,128]{2,1,0:T(8,128)(2,1)S(1)}, bf16[64,256,128]{2,1,0:T(8,128)(2,1)S(1)}, f32[19872,128]{1,0:T(8,128)S(1)}, f32[9,64,64]{2,1,0:T(8,128)S(1)}, f32[16,256]{1,0:T(8,128)S(1)}) custom-call(bf16[64,256,128]{2,1,0:T(8,128)(2,1)} %cot_hbm.1, bf16[64,256,128]{2,1,0:T(8,128)(2,1)} %pm_hbm.1, bf16[16,256]{1,0:T(8,128)(2,1)} %feat.1, ...), custom_call_target="tpu_custom_call" | custom-call | flops 7650410496 | bytes 16777216 | tf_op jit(solution)/shard_map/pallas_call | solution.py:624
  46.4 0.0 copy-done
  46.4 4.0 %shard_map.112 = (bf16[64,256,128]{2,1,0:T(8,128)(2,1)}, bf16[64,256,128]{2,1,0:T(8,128)(2,1)}, f32[9,64,64]{2,1,0:T(8,128)}, f32[16,256]{1,0:T(8,128)}) custom-call(bf16[64,256,128]{2,1,0:T(8,128)(2,1)S(1)} %get-tuple-element.13.hid_n, bf16[64,256,128]{2,1,0:T(8,128)(2,1)S(1)} %get-tuple-element.14.pg_n, f32[19872,128]{1,0:T(8,128)S(1)} %get-tuple-element.15.gt, ...), custom_call_target="tpu_custom_call" | custom-call | flops 4194304 | bytes 8388608 | tf_op jit(solution)/shard_map/pallas_call | solution.py:646
Async XLA Ops:
  0.6 45.8 %copy-start = (f32[64]{0:T(128)S(1)}, f32[64]{0:T(128)}, u32[]{:S(2)}) copy-start(f32[64]{0:T(128)} %bias.1) | copy-start | bytes 772

commit v6 on v5

--- a/solution.py
+++ b/solution.py
@@ -14,7 +14,7 @@
 NT = (((1,), (1,)), ((), ()))
 PACK = 16
 BLOCK = 32
-STEP = 4
+STEP = 16
 
 
 def dot(a, b, dims=None):
@@ -27,7 +27,7 @@
     nr, nc, ch, ti, outer, comm, residues,
     cot_hbm, pm_hbm, feat, lw, rw, ow, cw,
     hid_n, cot_n, gt, wg_out, fg_out,
-    slope_n, wide, cot_t, act_t, hx, terms, even, odd, upd_even, upd_odd, packs, land_row, land_col,
+    slope_n, wide, cot_t, act_t, hx, terms, even, odd, packs, land_row, land_col,
     lr, left_in, right_in, left, left_t, mixf, mix, wf, wb, ow_q, ow_t, mgf,
     wg_acc, wgs, land_a, land_b, fin, lg_acc, lg_out, rg_out, land_l, land_r,
     in_sem, f_send, f_recv, h_send, h_recv, w_send, w_recv, g_send, g_recv,
@@ -47,17 +47,6 @@
     cstep = 8
     nchunk = ch // cstep
 
-    cot_in = [
-        pltpu.make_async_copy(
-            cot_hbm.at[pl.ds(k * cstep, cstep)], cot_n.at[pl.ds(k * cstep, cstep)], in_sem.at[k]
-        )
-        for k in range(nchunk)
-    ]
-    pm_in = pltpu.make_async_copy(pm_hbm, hid_n, in_sem.at[nchunk])
-    for copy in cot_in:
-        copy.start()
-    pm_in.start()
-
     def source(k):
         f = col * nr + k
         return f // nc, lax.rem(f, nc)
@@ -85,6 +74,17 @@
             greet_unless_me(*source(k))
         total_greets = (nc - 1) + (nr - 1) + 4 + 2 * nr - jnp.where(goal == col, 2, 0)
 
+    cot_in = [
+        pltpu.make_async_copy(
+            cot_hbm.at[pl.ds(k * cstep, cstep)], cot_n.at[pl.ds(k * cstep, cstep)], in_sem.at[k]
+        )
+        for k in range(nchunk)
+    ]
+    pm_in = pltpu.make_async_copy(pm_hbm, hid_n, in_sem.at[nchunk])
+    for copy in cot_in:
+        copy.start()
+    pm_in.start()
+
     lr[...] = jnp.concatenate(
         [dot(feat[...], lw[...], NT), dot(feat[...], rw[...], NT), jnp.zeros((own, 128 - 2 * outer), F32)],
         axis=1,
@@ -95,22 +95,25 @@
             src_ref=src, dst_ref=dst, send_sem=ssem, recv_sem=rsem, device_id=dev, device_id_type=MESH
         )
 
+    def drain(blocks, sem):
+        pltpu.make_async_copy(blocks, blocks, sem).wait()
+
+    def drain_some(blocks, sem, one_less):
+        @pl.when(one_less)
+        def _():
+            drain(blocks.at[pl.ds(0, blocks.shape[0] - 1)], sem)
+
+        @pl.when(jnp.logical_not(one_less))
+        def _():
+            drain(blocks, sem)
+
     left_in[col] = lr[...]
-    left_moves, right_moves = [], []
     if comm:
         pl.semaphore_wait(barrier, total_greets)
-        for d in range(1, nc):
-            move = remote(
-                lr, left_in.at[col], f_send.at[d], f_recv.at[d], (row, lax.rem(col + d, nc))
-            )
-            move.start()
-            left_moves.append(move)
         for k in range(nr):
             me = jnp.logical_and(row == k, goal == col)
-            far = remote(
-                lr, right_in.at[slot], f_send.at[nc + k], f_recv.at[nc + slot], (k, goal)
-            )
-            near = pltpu.make_async_copy(lr, right_in.at[slot], f_recv.at[nc + slot])
+            far = remote(lr, right_in.at[slot], f_send.at[1], f_recv.at[1], (k, goal))
+            near = pltpu.make_async_copy(lr, right_in.at[slot], f_recv.at[1])
 
             @pl.when(me)
             def _():
@@ -120,7 +123,10 @@
             def _():
                 far.start()
 
-            right_moves.append((me, far))
+        for d in range(1, nc):
+            remote(
+                lr, left_in.at[col], f_send.at[0], f_recv.at[0], (row, lax.rem(col + d, nc))
+            ).start()
 
     for a in range(3):
         wf[a * ch : (a + 1) * ch, :] = jnp.concatenate([cw[3 * a + b] for b in range(3)], axis=1)
@@ -136,7 +142,7 @@
         for k in range(nchunk):
             cot_in[k].wait()
 
-            @pl.loop(0, cstep, unroll=2)
+            @pl.loop(0, cstep, unroll=8)
             def _(c):
                 at = pl.multiple_of((k * cstep + c) * pitch, 8)
                 wide[pl.ds(at, ti), :] = cot_n[k * cstep + c].astype(F32)
@@ -147,7 +153,7 @@
     window = lax.rem(lane + 4, 128) // 8
 
     def to_rows(dst, first, which, read):
-        @pl.loop(0, kg, unroll=2)
+        @pl.loop(0, kg, unroll=4)
         def _(k):
             packed = None
             for m in range(PACK):
@@ -171,7 +177,7 @@
             (edges.at[kg - 1], from_west.at[0], (down, east)),
         ]
         return [
-            remote(s, d, h_send.at[which, m], h_recv.at[which, m], dev)
+            remote(s, d, h_send.at[which, min(m // 2, 1)], h_recv.at[which, min(m // 2, 1)], dev)
             for m, (s, d, dev) in enumerate(plan)
         ]
 
@@ -182,10 +188,8 @@
             move.start()
 
     if comm:
-        for d in range(1, nc):
-            left_moves[d - 1].wait_recv()
-        for k in range(nr):
-            pltpu.make_async_copy(lr, right_in.at[k], f_recv.at[nc + k]).wait()
+        drain(left_in.at[pl.ds(0, nc - 1)], f_recv.at[0])
+        drain(right_in, f_recv.at[1])
     left[...] = left_in[...].reshape(nc * own, 128)[:, :outer]
     left_t[...] = left[...].astype(F32).T.astype(BF)
     right = right_in[...].reshape(nr * own, 128)[:, outer : 2 * outer]
@@ -214,14 +218,11 @@
                 slope_n[c + k] = e.astype(BF)
                 wide[pl.ds(c + k, ti, stride=wch), :] = jnp.maximum(h, e - 1.0)
 
-        upd_even[...] = update(0)
-
-        @pl.loop(0, ch, step=4)
+        @pl.loop(0, ch, step=16)
         def _(c):
-            upd_odd[...] = update(c + 2)
-            finish(c, upd_even[...])
-            upd_even[...] = update(jnp.minimum(c + 4, ch - 2))
-            finish(c + 2, upd_odd[...])
+            changes = [update(c + 2 * k) for k in range(8)]
+            for k in range(8):
+                finish(c + 2 * k, changes[k])
 
     p_hidden()
 
@@ -287,8 +288,8 @@
                 gt[at, :] = gt[at, :] + term if s < 2 else term
 
     if comm:
-        for move in cot_moves:
-            move.wait_recv()
+        drain(land_row.at[0], h_recv.at[0, 0])
+        drain(land_col.at[0], h_recv.at[0, 1])
     unpack_edges(cot_t, 0, 0)
     gt[: 8 * wch] = jnp.zeros((8 * wch, 128), F32)
     wg_acc[...] = jnp.zeros_like(wg_acc)
@@ -338,9 +339,8 @@
         a, b = k // 3, k % 3
         tap = wg_acc[b * ch : (b + 1) * ch, a * ch : (a + 1) * ch]
         wgs[k] = jnp.concatenate([tap[:half], tap[half:]], axis=1).astype(BF)
-    a_moves, b_moves, c_moves, l_moves, r_moves = [], [], [], [], []
     for k, c in enumerate(owners):
-        move = remote(wgs.at[k], land_a.at[col], w_send.at[k], w_recv.at[col], (row, c))
+        move = remote(wgs.at[k], land_a.at[col], w_send.at[0], w_recv.at[0], (row, c))
 
         @pl.when(col == c)
         def _():
@@ -352,7 +352,6 @@
             def _():
                 move.start()
 
-            a_moves.append((c, move))
 
     p_back()
 
@@ -362,42 +361,23 @@
             total = total + refs[k].astype(F32)
         return total
 
-    for d in range(1, nr):
-        b_moves.append(
-            remote(
-                land_b.at[row], land_b.at[row], w_send.at[taps + d], w_recv.at[nc + d],
-                (lax.rem(row + d, nr), col),
-            )
-        )
-    for d in range(1, nc):
-        c_moves.append(
-            remote(
-                fin.at[mine], fin.at[mine], w_send.at[taps + nr + d], w_recv.at[nc + nr + mine],
-                (row, lax.rem(col + d, nc)),
-            )
-        )
-
     @pl.when(is_owner)
     def _():
         if comm:
-            for c in range(nc):
-
-                @pl.when(col != c)
-                def _():
-                    pltpu.make_async_copy(wgs.at[0], land_a.at[c], w_recv.at[c]).wait()
-
+            drain(land_a.at[pl.ds(0, nc - 1)], w_recv.at[0])
         land_b[row] = each(land_a)
         if comm:
-            for move in b_moves:
-                move.start()
+            for d in range(1, nr):
+                to = (lax.rem(row + d, nr), col)
+                remote(land_b.at[row], land_b.at[row], w_send.at[1], w_recv.at[1], to).start()
 
     lg_acc[...] = jnp.zeros_like(lg_acc)
 
     def p_grad():
-        @pl.loop(0, ch, step=8)
+        @pl.loop(0, ch, step=16)
         def _(c):
             lg = 0
-            for half in (c, c + 4):
+            for half in (c, c + 4, c + 8, c + 12):
                 grads = []
                 for m in range(4):
                     g = gt[pl.ds(8 * wch + half + m, ti, stride=wch), :]
@@ -424,16 +404,14 @@
     if comm:
         for d in range(1, nc):
             other = lax.rem(col + d, nc)
-            move = remote(lg_out.at[other], land_l.at[col], g_send.at[d], g_recv.at[d], (row, other))
-            move.start()
-            l_moves.append(move)
+            remote(
+                lg_out.at[other], land_l.at[col], g_send.at[0], g_recv.at[0], (row, other)
+            ).start()
         for k in range(nr):
             r, c = source(k)
             me = jnp.logical_and(r == row, c == col)
-            far = remote(
-                rg_out.at[k], land_r.at[row], g_send.at[nc + k], g_recv.at[nc + row], (r, c)
-            )
-            near = pltpu.make_async_copy(rg_out.at[k], land_r.at[row], g_recv.at[nc + row])
+            far = remote(rg_out.at[k], land_r.at[row], g_send.at[1], g_recv.at[1], (r, c))
+            near = pltpu.make_async_copy(rg_out.at[k], land_r.at[row], g_recv.at[1])
 
             @pl.when(me)
             def _():
@@ -443,21 +421,19 @@
             def _():
                 far.start()
 
-            r_moves.append((me, far))
-
     @pl.when(is_owner)
     def _():
         if comm:
-            for move in b_moves:
-                move.wait_recv()
+            drain(land_b.at[pl.ds(0, nr - 1)], w_recv.at[1])
         fin[mine] = (each(land_b) * (1.0 / residues)).astype(BF)
         if comm:
-            for move in c_moves:
-                move.start()
-
-    if comm:
-        for move in act_moves:
-            move.wait_recv()
+            for d in range(1, nc):
+                to = (row, lax.rem(col + d, nc))
+                remote(fin.at[mine], fin.at[mine], w_send.at[2], w_recv.at[2], to).start()
+
+    if comm:
+        drain(land_row.at[1], h_recv.at[1, 0])
+        drain(land_col.at[1], h_recv.at[1, 1])
     unpack_edges(act_t, 4, 1)
     gt[: 8 * wch] = jnp.zeros((8 * wch, 128), F32)
 
@@ -478,10 +454,8 @@
     spread(halves(dot(wf[...], even[...])), ng, (2, 1, 0))
 
     if comm:
-        for move in l_moves:
-            move.wait_recv()
-        for k in range(nr):
-            pltpu.make_async_copy(rg_out.at[k], land_r.at[k], g_recv.at[nc + k]).wait()
+        drain(land_l.at[pl.ds(0, nc - 1)], g_recv.at[0])
+        drain(land_r, g_recv.at[1])
     lg = land_l[0]
     for k in range(1, nc):
         lg = lg + land_l[k]
@@ -499,35 +473,26 @@
 
     fg_out[...] = (exact(lg, lw[...]) + exact(rg, rw[...])) * (1.0 / math.sqrt(residues))
 
-    for k, c in enumerate(owners):
-        if comm:
-
-            @pl.when(col != c)
-            def _():
-                pltpu.make_async_copy(wgs.at[0], fin.at[k], w_recv.at[nc + nr + k]).wait()
-
+    if comm:
+        drain_some(fin, w_recv.at[2], is_owner)
+    for k in range(taps):
         tap = fin[k].astype(F32)
         wg_out[k] = jnp.concatenate([tap[:, :ch], tap[:, ch:]], axis=0)
 
     if comm:
-        for move in left_moves + cot_moves + act_moves + l_moves:
-            move.wait_send()
-        for c, move in a_moves:
-
-            @pl.when(col != c)
-            def _():
-                move.wait_send()
+        drain(left_in.at[pl.ds(0, nc - 1)], f_send.at[0])
+        drain_some(right_in, f_send.at[1], goal == col)
+        for which in range(2):
+            drain(land_row.at[which], h_send.at[which, 0])
+            drain(land_col.at[which], h_send.at[which, 1])
+        drain_some(wgs, w_send.at[0], is_owner)
+        drain(land_l.at[pl.ds(0, nc - 1)], g_send.at[0])
+        drain_some(land_r, g_send.at[1], goal == col)
 
         @pl.when(is_owner)
         def _():
-            for move in b_moves + c_moves:
-                move.wait_send()
-
-        for me, far in right_moves + r_moves:
-
-            @pl.when(jnp.logical_not(me))
-            def _():
-                far.wait_send()
+            drain(land_b.at[pl.ds(0, nr - 1)], w_send.at[1])
+            drain(land_a.at[pl.ds(0, nc - 1)], w_send.at[2])
 
 
 def last_kernel(
@@ -583,8 +548,6 @@
         V((ti // 8 + 1, 3 * ch, 1024), BF),
         V((3 * ch, 1024), BF),
         V((3 * ch, 1024), BF),
-        V((ti, 256), F32),
-        V((ti, 256), F32),
         V((2, kg, ch, 128), BF),
         V((2, 2, 4, ch, 128), BF),
         V((2, 2, kg + 2, ch, 128), BF),
@@ -611,14 +574,14 @@
         V((nc, own, outer), F32),
         V((nr, own, outer), F32),
         dma((ch // 8 + 1,)),
-        dma((nc + nr,)),
-        dma((nc + nr,)),
-        dma((2, 8)),
-        dma((2, 8)),
-        dma((9 + nr + nc,)),
-        dma((nc + nr + 9,)),
-        dma((nc + nr,)),
-        dma((nc + nr,)),
+        dma((2,)),
+        dma((2,)),
+        dma((2, 2)),
+        dma((2, 2)),
+        dma((3,)),
+        dma((3,)),
+        dma((2,)),
+        dma((2,)),
     ]
     macs = ti * tj * (27 * ch * ch + 3 * outer * ch)
     out = pl.pallas_call(

time: 50.6 us -> 51.5 us (1.018)
  no operation moved by 1% of the time
where the time goes in v6:
time: 51.5 us; the launch traced here: 50.9 us
  Pallas kernels  50.1 us (97%)
  between operations  0.82 us (2%)
    pallas_call x1, Pallas kernels, call(): pl.pallas_call(functools.partial(kernel, nr, nc, ch, ti, outer, comm, res...  46.1 us
    pallas_call x1, Pallas kernels, call(): pl.pallas_call(last_kernel, out_shape=[jax.ShapeDtypeStruct((ch, ti, tj),...  4.03 us

profile of v6, /device:TPU:0, one launch (start us, length us, event | category | flops | bytes accessed | tf_op | source)
XLA Modules:
  0.0 50.9 jit_solution(8956940721822044766)
XLA Ops:
  0.6 0.0 copy-start
  0.6 46.1 %shard_map.111 = (bf16[64,256,128]{2,1,0:T(8,128)(2,1)S(1)}, bf16[64,256,128]{2,1,0:T(8,128)(2,1)S(1)}, f32[19872,128]{1,0:T(8,128)S(1)}, f32[9,64,64]{2,1,0:T(8,128)S(1)}, f32[16,256]{1,0:T(8,128)S(1)}) custom-call(bf16[64,256,128]{2,1,0:T(8,128)(2,1)} %cot_hbm.1, bf16[64,256,128]{2,1,0:T(8,128)(2,1)} %pm_hbm.1, bf16[16,256]{1,0:T(8,128)(2,1)} %feat.1, ...), custom_call_target="tpu_custom_call" | custom-call | flops 7650410496 | bytes 16777216 | tf_op jit(solution)/shard_map/pallas_call | solution.py:587
  46.7 0.0 copy-done
  46.7 4.0 %shard_map.112 = (bf16[64,256,128]{2,1,0:T(8,128)(2,1)}, bf16[64,256,128]{2,1,0:T(8,128)(2,1)}, f32[9,64,64]{2,1,0:T(8,128)}, f32[16,256]{1,0:T(8,128)}) custom-call(bf16[64,256,128]{2,1,0:T(8,128)(2,1)S(1)} %get-tuple-element.13.hid_n, bf16[64,256,128]{2,1,0:T(8,128)(2,1)S(1)} %get-tuple-element.14.pg_n, f32[19872,128]{1,0:T(8,128)S(1)} %get-tuple-element.15.gt, ...), custom_call_target="tpu_custom_call" | custom-call | flops 4194304 | bytes 8388608 | tf_op jit(solution)/shard_map/pallas_call | solution.py:609
Async XLA Ops:
  0.6 46.1 %copy-start = (f32[64]{0:T(128)S(1)}, f32[64]{0:T(128)}, u32[]{:S(2)}) copy-start(f32[64]{0:T(128)} %bias.1) | copy-start | bytes 772

commit v7 on v6

--- a/solution.py
+++ b/solution.py
@@ -14,7 +14,7 @@
 NT = (((1,), (1,)), ((), ()))
 PACK = 16
 BLOCK = 32
-STEP = 16
+STEP = 4
 
 
 def dot(a, b, dims=None):
@@ -152,29 +152,37 @@
     lane = lax.broadcasted_iota(jnp.int32, (ch, 128), 1)
     window = lax.rem(lane + 4, 128) // 8
 
+    first_four = lax.rem(lane, 8) < 4
+    kt = kg // 2
+
     def to_rows(dst, first, which, read):
-        @pl.loop(0, kg, unroll=4)
-        def _(k):
-            packed = None
-            for m in range(PACK):
-                row_at = PACK * k + m
-                x = read(row_at).astype(BF)
-                dst[first + row_at] = x
-                packed = x if m == 0 else jnp.where(window == m, pltpu.roll(x, 8 * m, 1), packed)
-            packs[which, k] = packed
+        @pl.loop(0, kt, unroll=min(4, kt))
+        def _(t):
+            lines = []
+            for k in range(2):
+                packed = None
+                for m in range(PACK):
+                    row_at = 2 * PACK * t + PACK * k + m
+                    x = read(row_at).astype(BF)
+                    dst[first + row_at] = x
+                    packed = x if m == 0 else jnp.where(window == m, pltpu.roll(x, 8 * m, 1), packed)
+                lines.append(packed)
+            moved = pltpu.roll(lines[1], 4, 1)
+            packs[which, 0, t] = jnp.where(first_four, lines[0], moved)
+            packs[which, 1, t] = jnp.where(first_four, moved, lines[0])
 
     def halo_moves(src, first, which):
-        edges = packs.at[which]
+        low, high = packs.at[which, 0], packs.at[which, 1]
         from_west, from_east = land_col.at[which, 0], land_col.at[which, 1]
         plan = [
             (src.at[pl.ds(first, 4)], land_row.at[which, 1], (up, col)),
             (src.at[pl.ds(first + ti - 4, 4)], land_row.at[which, 0], (down, col)),
-            (edges, from_east.at[pl.ds(1, kg)], (row, west)),
-            (edges, from_west.at[pl.ds(1, kg)], (row, east)),
-            (edges.at[0], from_east.at[kg + 1], (up, west)),
-            (edges.at[0], from_west.at[kg + 1], (up, east)),
-            (edges.at[kg - 1], from_east.at[0], (down, west)),
-            (edges.at[kg - 1], from_west.at[0], (down, east)),
+            (low, from_east.at[pl.ds(1, kt)], (row, west)),
+            (high, from_west.at[pl.ds(1, kt)], (row, east)),
+            (low.at[0], from_east.at[kt + 1], (up, west)),
+            (high.at[0], from_west.at[kt + 1], (up, east)),
+            (low.at[kt - 1], from_east.at[0], (down, west)),
+            (high.at[kt - 1], from_west.at[0], (down, east)),
         ]
         return [
             remote(s, d, h_send.at[which, min(m // 2, 1)], h_recv.at[which, min(m // 2, 1)], dev)
@@ -243,19 +251,20 @@
         dst[first : first + 4] = keep(has_up, land_row[which, 0])
         dst[first + ti + 4 : first + ti + 8] = keep(has_down, land_row[which, 1])
 
-        def place(k, ok):
-            from_west = keep(jnp.logical_and(ok, has_west), land_col[which, 0, k])
-            from_east = keep(jnp.logical_and(ok, has_east), land_col[which, 1, k])
-            hx[k] = jnp.where(
-                lax.rem(lane, 8) < 4, pltpu.roll(from_west, 4, 1), pltpu.roll(from_east, 124, 1)
+        def place(t, ok):
+            from_west = keep(jnp.logical_and(ok, has_west), land_col[which, 0, t])
+            from_east = keep(jnp.logical_and(ok, has_east), land_col[which, 1, t])
+            return (
+                jnp.where(first_four, pltpu.roll(from_west, 4, 1), pltpu.roll(from_east, 124, 1)),
+                jnp.where(first_four, from_west, pltpu.roll(from_east, 120, 1)),
             )
 
-        place(0, has_up)
-        place(kg + 1, has_down)
-
-        @pl.loop(1, kg + 1, unroll=4)
-        def _(k):
-            place(k, True)
+        hx[0] = place(0, has_up)[1]
+        hx[kg + 1] = place(kt + 1, has_down)[0]
+
+        @pl.loop(1, kt + 1, unroll=min(4, kt))
+        def _(t):
+            hx[2 * t - 1], hx[2 * t] = place(t, True)
 
     def fill(dst, src, first, n, q, turned):
         for r in range(8):
@@ -548,9 +557,9 @@
         V((ti // 8 + 1, 3 * ch, 1024), BF),
         V((3 * ch, 1024), BF),
         V((3 * ch, 1024), BF),
-        V((2, kg, ch, 128), BF),
+        V((2, 2, kg // 2, ch, 128), BF),
         V((2, 2, 4, ch, 128), BF),
-        V((2, 2, kg + 2, ch, 128), BF),
+        V((2, 2, kg // 2 + 2, ch, 128), BF),
         V((own, 128), BF),
         V((nc, own, 128), BF),
         V((nr, own, 128), BF),

time: 51.5 us -> 46.9 us (0.911)
  Pallas kernels: 50.1 us -> 46.1 us
    pallas_call x1, Pallas kernels: 46.1 us -> 42 us  [call(): pl.pallas_call(functools.partial(kernel, nr, nc, ch, ti, outer, comm, res...]
where the time goes in v7:
time: 46.9 us; the launch traced here: 46.7 us
  Pallas kernels  46.1 us (98%)
  between operations  0.66 us (1%)
    pallas_call x1, Pallas kernels, call(): pl.pallas_call(functools.partial(kernel, nr, nc, ch, ti, outer, comm, res...  42 us
    pallas_call x1, Pallas kernels, call(): pl.pallas_call(last_kernel, out_shape=[jax.ShapeDtypeStruct((ch, ti, tj),...  4.03 us

profile of v7, /device:TPU:0, one launch (start us, length us, event | category | flops | bytes accessed | tf_op | source)
XLA Modules:
  0.0 46.7 jit_solution(2444987952231717021)
XLA Ops:
  0.6 0.0 copy-start
  0.6 42.0 %shard_map.111 = (bf16[64,256,128]{2,1,0:T(8,128)(2,1)S(1)}, bf16[64,256,128]{2,1,0:T(8,128)(2,1)S(1)}, f32[19872,128]{1,0:T(8,128)S(1)}, f32[9,64,64]{2,1,0:T(8,128)S(1)}, f32[16,256]{1,0:T(8,128)S(1)}) custom-call(bf16[64,256,128]{2,1,0:T(8,128)(2,1)} %cot_hbm.1, bf16[64,256,128]{2,1,0:T(8,128)(2,1)} %pm_hbm.1, bf16[16,256]{1,0:T(8,128)(2,1)} %feat.1, ...), custom_call_target="tpu_custom_call" | custom-call | flops 7650410496 | bytes 16777216 | tf_op jit(solution)/shard_map/pallas_call | solution.py:596
  42.7 0.0 copy-done
  42.7 4.0 %shard_map.112 = (bf16[64,256,128]{2,1,0:T(8,128)(2,1)}, bf16[64,256,128]{2,1,0:T(8,128)(2,1)}, f32[9,64,64]{2,1,0:T(8,128)}, f32[16,256]{1,0:T(8,128)}) custom-call(bf16[64,256,128]{2,1,0:T(8,128)(2,1)S(1)} %get-tuple-element.13.hid_n, bf16[64,256,128]{2,1,0:T(8,128)(2,1)S(1)} %get-tuple-element.14.pg_n, f32[19872,128]{1,0:T(8,128)S(1)} %get-tuple-element.15.gt, ...), custom_call_target="tpu_custom_call" | custom-call | flops 4194304 | bytes 8388608 | tf_op jit(solution)/shard_map/pallas_call | solution.py:618
Async XLA Ops:
  0.6 42.1 %copy-start = (f32[64]{0:T(128)S(1)}, f32[64]{0:T(128)}, u32[]{:S(2)}) copy-start(f32[64]{0:T(128)} %bias.1) | copy-start | bytes 772

commit v8 on v7

--- a/solution.py
+++ b/solution.py
@@ -14,7 +14,7 @@
 NT = (((1,), (1,)), ((), ()))
 PACK = 16
 BLOCK = 32
-STEP = 4
+STEP = 8
 
 
 def dot(a, b, dims=None):

time: 46.9 us -> 46 us (0.981)
  Pallas kernels: 46.1 us -> 45 us
    pallas_call x1, Pallas kernels: 42 us -> 41 us  [call(): pl.pallas_call(functools.partial(kernel, nr, nc, ch, ti, outer, comm, res...]
where the time goes in v8:
time: 46 us; the launch traced here: 45.8 us
  Pallas kernels  45 us (98%)
  between operations  0.82 us (2%)
    pallas_call x1, Pallas kernels, call(): pl.pallas_call(functools.partial(kernel, nr, nc, ch, ti, outer, comm, res...  41 us
    pallas_call x1, Pallas kernels, call(): pl.pallas_call(last_kernel, out_shape=[jax.ShapeDtypeStruct((ch, ti, tj),...  4.03 us

profile of v8, /device:TPU:0, one launch (start us, length us, event | category | flops | bytes accessed | tf_op | source)
XLA Modules:
  0.0 45.8 jit_solution(7034337226228031785)
XLA Ops:
  0.6 0.0 copy-start
  0.6 41.0 %shard_map.111 = (bf16[64,256,128]{2,1,0:T(8,128)(2,1)S(1)}, bf16[64,256,128]{2,1,0:T(8,128)(2,1)S(1)}, f32[19872,128]{1,0:T(8,128)S(1)}, f32[9,64,64]{2,1,0:T(8,128)S(1)}, f32[16,256]{1,0:T(8,128)S(1)}) custom-call(bf16[64,256,128]{2,1,0:T(8,128)(2,1)} %cot_hbm.1, bf16[64,256,128]{2,1,0:T(8,128)(2,1)} %pm_hbm.1, bf16[16,256]{1,0:T(8,128)(2,1)} %feat.1, ...), custom_call_target="tpu_custom_call" | custom-call | flops 7650410496 | bytes 16777216 | tf_op jit(solution)/shard_map/pallas_call | solution.py:596
  41.6 0.0 copy-done
  41.7 4.0 %shard_map.112 = (bf16[64,256,128]{2,1,0:T(8,128)(2,1)}, bf16[64,256,128]{2,1,0:T(8,128)(2,1)}, f32[9,64,64]{2,1,0:T(8,128)}, f32[16,256]{1,0:T(8,128)}) custom-call(bf16[64,256,128]{2,1,0:T(8,128)(2,1)S(1)} %get-tuple-element.13.hid_n, bf16[64,256,128]{2,1,0:T(8,128)(2,1)S(1)} %get-tuple-element.14.pg_n, f32[19872,128]{1,0:T(8,128)S(1)} %get-tuple-element.15.gt, ...), custom_call_target="tpu_custom_call" | custom-call | flops 4194304 | bytes 8388608 | tf_op jit(solution)/shard_map/pallas_call | solution.py:618
Async XLA Ops:
  0.6 41.0 %copy-start = (f32[64]{0:T(128)S(1)}, f32[64]{0:T(128)}, u32[]{:S(2)}) copy-start(f32[64]{0:T(128)} %bias.1) | copy-start | bytes 772

commit v9 on v8

--- a/solution.py
+++ b/solution.py
@@ -142,10 +142,10 @@
         for k in range(nchunk):
             cot_in[k].wait()
 
-            @pl.loop(0, cstep, unroll=8)
-            def _(c):
-                at = pl.multiple_of((k * cstep + c) * pitch, 8)
-                wide[pl.ds(at, ti), :] = cot_n[k * cstep + c].astype(F32)
+        @pl.loop(0, ch, unroll=8)
+        def _(c):
+            at = pl.multiple_of(c * pitch, 8)
+            wide[pl.ds(at, ti), :] = cot_n[c].astype(F32)
 
     p_widen()
 
@@ -404,9 +404,7 @@
     p_grad()
 
     mg = jnp.concatenate([mgf[p * wch : p * wch + ch, :] for p in range(outer)], axis=0)
-    mg_hi = mg.astype(BF)
-    mg_lo = (mg - mg_hi.astype(F32)).astype(BF)
-    rg = (dot(ow_q[...], mg_hi) + dot(ow_q[...], mg_lo)).T
+    rg = dot(ow_q[...], mg.astype(BF)).T
     rg_out[...] = rg.reshape(nr, own, outer)
     lg_out[...] = lg_acc[...].T.reshape(nc, own, outer)
     land_l[col] = lg_out[col]

time: 46 us -> 45.9 us (level)
  no operation moved by 1% of the time
where the time goes in v9:
time: 45.9 us; the launch traced here: 45.8 us
  Pallas kernels  45 us (98%)
  between operations  0.82 us (2%)
    pallas_call x1, Pallas kernels, call(): pl.pallas_call(functools.partial(kernel, nr, nc, ch, ti, outer, comm, res...  40.9 us
    pallas_call x1, Pallas kernels, call(): pl.pallas_call(last_kernel, out_shape=[jax.ShapeDtypeStruct((ch, ti, tj),...  4.03 us

profile of v9, /device:TPU:0, one launch (start us, length us, event | category | flops | bytes accessed | tf_op | source)
XLA Modules:
  0.0 45.8 jit_solution(12462203853249145534)
XLA Ops:
  0.6 0.0 copy-start
  0.6 40.9 %shard_map.111 = (bf16[64,256,128]{2,1,0:T(8,128)(2,1)S(1)}, bf16[64,256,128]{2,1,0:T(8,128)(2,1)S(1)}, f32[19872,128]{1,0:T(8,128)S(1)}, f32[9,64,64]{2,1,0:T(8,128)S(1)}, f32[16,256]{1,0:T(8,128)S(1)}) custom-call(bf16[64,256,128]{2,1,0:T(8,128)(2,1)} %cot_hbm.1, bf16[64,256,128]{2,1,0:T(8,128)(2,1)} %pm_hbm.1, bf16[16,256]{1,0:T(8,128)(2,1)} %feat.1, ...), custom_call_target="tpu_custom_call" | custom-call | flops 7650410496 | bytes 16777216 | tf_op jit(solution)/shard_map/pallas_call | solution.py:594
  41.6 0.0 copy-done
  41.6 4.0 %shard_map.112 = (bf16[64,256,128]{2,1,0:T(8,128)(2,1)}, bf16[64,256,128]{2,1,0:T(8,128)(2,1)}, f32[9,64,64]{2,1,0:T(8,128)}, f32[16,256]{1,0:T(8,128)}) custom-call(bf16[64,256,128]{2,1,0:T(8,128)(2,1)S(1)} %get-tuple-element.13.hid_n, bf16[64,256,128]{2,1,0:T(8,128)(2,1)S(1)} %get-tuple-element.14.pg_n, f32[19872,128]{1,0:T(8,128)S(1)} %get-tuple-element.15.gt, ...), custom_call_target="tpu_custom_call" | custom-call | flops 4194304 | bytes 8388608 | tf_op jit(solution)/shard_map/pallas_call | solution.py:616
Async XLA Ops:
  0.6 41.0 %copy-start = (f32[64]{0:T(128)S(1)}, f32[64]{0:T(128)}, u32[]{:S(2)}) copy-start(f32[64]{0:T(128)} %bias.1) | copy-start | bytes 772
